TPU v7x, 512 devices: a whole 4x4x16 slice. The times are simulated.
512 devices in a mesh: lat: 16 (over z_lo, core), lon: 32 (over z_hi, x, y).
Axes of the slice: x: 4, y: 4, z: 16 (z_hi: 2, z_lo: 8; z = z_hi * 8 + z_lo), core: 2. Of those that a mesh axis runs over, the one named last changes fastest.
Arguments:
- fields: float32 [2, 2, 192, 192, 192], P(None, None, 'lat', 'lon'), may hold values from -60 to 60
- cotangent: float32 [2, 2, 192, 192, 192], P(None, None, 'lat', 'lon'), may hold values from -0.75 to 0.75
- keep_mask: int32 [2, 2], replicated, may hold values from 0 to 1, as said below
- region_ids: int32 [2, 192, 192], P(None, 'lat', 'lon'), may hold values from 0 to 2
- norm1_gain: float32 [192], replicated, may hold values from 0.25 to 1.75
- norm1_shift: float32 [192], replicated, may hold values from -3 to 3
- qkv_weight: float32 [192, 576], replicated, may hold values from -0.4375 to 0.4375
- qkv_bias: float32 [576], replicated, may hold values from -3 to 3
- position_table: float32 [16, 6, 6336], P('lat'), may hold values from -4 to 410
- proj_weight: float32 [192, 192], replicated, may hold values from -0.4375 to 0.4375
- proj_bias: float32 [192], replicated, may hold values from -3 to 3
- norm2_gain: float32 [192], replicated, may hold values from 0.25 to 1.75
- norm2_shift: float32 [192], replicated, may hold values from -3 to 3
- mlp_in_weight: float32 [192, 768], replicated, may hold values from -0.4375 to 0.4375
- mlp_in_bias: float32 [768], replicated, may hold values from -3 to 3
- mlp_out_weight: float32 [768, 192], replicated, may hold values from -0.21875 to 0.21875
Outputs:
- fields_grad: float32 [2, 2, 192, 192, 192], P(None, None, 'lat', 'lon')
- norm1_gain_grad: float32 [192], replicated
- norm1_shift_grad: float32 [192], replicated
- qkv_weight_grad: float32 [192, 576], P('lon')
- qkv_bias_grad: float32 [576], replicated
- table_grad: float32 [16, 6, 6336], P('lat')
- proj_weight_grad: float32 [192, 192], P('lon')
- proj_bias_grad: float32 [192], replicated
- norm2_gain_grad: float32 [192], replicated
- norm2_shift_grad: float32 [192], replicated
- mlp_in_weight_grad: float32 [192, 768], P('lon')
- mlp_in_bias_grad: float32 [768], replicated
- mlp_out_weight_grad: float32 [768, 192], P('lon')
Inputs may be any that keep to these rules, and one draw needn't show every extreme that they name: `keep_mask`: each of the two columns holds at least one 1 and at least one 0.
All inputs are finite; a program needn't handle non-finite values.
Results may differ from a plain program's by a relative error of at most 0.00013.
Values sent between devices are 32-bit elements; how exact they have to be, the bound alone decides.
A program may use at most 128 MiB of HBM per device.

v0:
```python
import math

import jax
import jax.numpy as jnp
from jax import lax
from jax.sharding import PartitionSpec as P

keep_rate = 0.8
norm_eps = 1e-05
top_precision = lax.Precision.HIGHEST


def passed_along(block, axis, distance):
    devices = range(lax.axis_size(axis))
    route = [((i - distance) % len(devices), i) for i in devices]
    return lax.ppermute(block, axis, route)


def layer_norm(values, norm_gain, norm_shift):
    center = values - jnp.mean(values, axis=-1, keepdims=True)
    spread = jnp.mean(center * center, axis=-1, keepdims=True)
    return center * lax.rsqrt(spread + norm_eps) * norm_gain + norm_shift


def position_bias(table_rows, levels_win, lat_rows, lon_cols):
    leading = table_rows.shape[:-1]
    relative = 2 * lon_cols - 1
    token_count = levels_win * lat_rows * lon_cols
    token_ids = jnp.arange(token_count, dtype=jnp.int32)
    level_of = token_ids // (lat_rows * lon_cols)
    row_of = token_ids // lon_cols % lat_rows
    col_of = token_ids % lon_cols
    position = (level_of[:, None] * levels_win + level_of[None, :]) * lat_rows + row_of[:, None]
    position = (
        (position * lat_rows + row_of[None, :]) * relative
        + col_of[:, None]
        - col_of[None, :]
        + lon_cols
        - 1
    )
    picked = jnp.take(table_rows, position.reshape(-1), axis=-1)
    return picked.reshape(leading + (token_count, token_count))


def attend(
    windows,
    qkv_weight,
    qkv_bias,
    table_rows,
    proj_weight,
    proj_bias,
    regions,
    levels_win,
    lat_rows,
    lon_cols,
):
    leading = windows.shape[:-2]
    token_count = windows.shape[-2]
    features = windows.shape[-1]
    head_count = table_rows.shape[-2]
    head_width = features // head_count
    projected = jnp.matmul(windows, qkv_weight, precision=top_precision) + qkv_bias
    projected = projected.reshape(leading + (token_count, 3, head_count, head_width))
    query_matrix = projected[..., 0, :, :]
    key_matrix = projected[..., 1, :, :]
    value_matrix = projected[..., 2, :, :]
    logit_scores = jnp.einsum(
        "...zjx,...pjx->...jzp", query_matrix, key_matrix, precision=top_precision
    ) / math.sqrt(head_width)
    logit_scores = logit_scores + position_bias(table_rows, levels_win, lat_rows, lon_cols)
    same_region = regions[..., :, None] == regions[..., None, :]
    logit_scores = jnp.where(same_region[..., None, :, :], logit_scores, -1e30)
    softmax_weights = jax.nn.softmax(logit_scores, axis=-1)
    merged_head_output = jnp.einsum(
        "...kwa,...aks->...wks", softmax_weights, value_matrix, precision=top_precision
    )
    merged_head_output = merged_head_output.reshape(leading + (token_count, features))
    return jnp.matmul(merged_head_output, proj_weight, precision=top_precision) + proj_bias


def mlp_branch(values, norm_gain, norm_shift, in_weight, in_bias, out_weight):
    normed = layer_norm(values, norm_gain, norm_shift)
    hidden = jax.nn.gelu(
        jnp.matmul(normed, in_weight, precision=top_precision) + in_bias, approximate=False
    )
    return jnp.matmul(hidden, out_weight, precision=top_precision)


def to_window(values):
    half_z = values.shape[-4] // 2
    half_h = values.shape[-3] // 2
    half_w = values.shape[-2] // 2
    values = jnp.roll(values, -half_z, axis=-4)
    upper_rows = passed_along(values[..., :half_h, :, :], "lat", -1)
    values = jnp.concatenate((values[..., half_h:, :, :], upper_rows), axis=-3)
    left_cols = passed_along(values[..., :half_w, :], "lon", -1)
    return jnp.concatenate((values[..., half_w:, :], left_cols), axis=-2)


def to_anchor(values):
    half_z = values.shape[-4] // 2
    half_h = values.shape[-3] // 2
    half_w = values.shape[-2] // 2
    right_cols = passed_along(values[..., half_w:, :], "lon", 1)
    values = jnp.concatenate((right_cols, values[..., :half_w, :]), axis=-2)
    lower_rows = passed_along(values[..., half_h:, :, :], "lat", 1)
    values = jnp.concatenate((lower_rows, values[..., :half_h, :, :]), axis=-3)
    return jnp.roll(values, half_z, axis=-4)


def per_device(
    fields,
    cotangent,
    keep_mask,
    region_ids,
    norm1_gain,
    norm1_shift,
    qkv_weight,
    qkv_bias,
    position_table,
    proj_weight,
    proj_bias,
    norm2_gain,
    norm2_shift,
    mlp_in_weight,
    mlp_in_bias,
    mlp_out_weight,
):
    batch_size, levels_win, lat_rows, lon_cols, features = fields.shape
    token_count = levels_win * lat_rows * lon_cols
    table_rows = position_table[0]
    regions = region_ids.reshape(token_count)
    keep_factor = keep_mask.astype(jnp.float32) / keep_rate
    keep_attn = keep_factor[:, 0].reshape(batch_size, 1, 1, 1, 1)
    keep_mlp = keep_factor[:, 1].reshape(batch_size, 1, 1, 1, 1)

    def attend_block(shifted, weight_in, bias_in, table_part, weight_out, bias_out):
        windows = shifted.reshape(batch_size, token_count, features)
        result = attend(
            windows,
            weight_in,
            bias_in,
            table_part,
            weight_out,
            bias_out,
            regions,
            levels_win,
            lat_rows,
            lon_cols,
        )
        return result.reshape(shifted.shape)

    normed, norm1_back = jax.vjp(layer_norm, fields, norm1_gain, norm1_shift)
    shifted = to_window(normed)
    branch, attend_back = jax.vjp(
        attend_block, shifted, qkv_weight, qkv_bias, table_rows, proj_weight, proj_bias
    )
    middle = fields + keep_attn * to_anchor(branch)
    mlp_back = jax.vjp(
        mlp_branch, middle, norm2_gain, norm2_shift, mlp_in_weight, mlp_in_bias, mlp_out_weight
    )[1]
    mlp_grads = mlp_back(keep_mlp * cotangent)
    middle_grad = cotangent + mlp_grads[0]
    attend_grads = attend_back(to_window(keep_attn * middle_grad))
    norm1_grads = norm1_back(to_anchor(attend_grads[0]))
    source_grad = middle_grad + norm1_grads[0]
    fields_grad, norm1_grads, attend_grads, mlp_grads = (
        source_grad,
        norm1_grads[1:],
        attend_grads[1:],
        mlp_grads[1:],
    )
    large_grads = (attend_grads[0], attend_grads[3], mlp_grads[2], mlp_grads[4])
    totals = lax.psum((large_grads[0], large_grads[1], large_grads[2], large_grads[3]), "lat")
    shares = (
        lax.psum_scatter(totals[0], "lon", scatter_dimension=0, tiled=True),
        lax.psum_scatter(totals[1], "lon", scatter_dimension=0, tiled=True),
        lax.psum_scatter(totals[2], "lon", scatter_dimension=0, tiled=True),
        lax.psum_scatter(totals[3], "lon", scatter_dimension=0, tiled=True),
    )
    small_sums = lax.psum(
        (
            norm1_grads[0],
            norm1_grads[1],
            attend_grads[1],
            attend_grads[4],
            mlp_grads[0],
            mlp_grads[1],
            mlp_grads[3],
        ),
        ("lat", "lon"),
    )
    table_total = lax.psum(attend_grads[2][None], "lon")
    return (
        fields_grad,
        small_sums[0],
        small_sums[1],
        shares[0],
        small_sums[2],
        table_total,
        shares[1],
        small_sums[3],
        small_sums[4],
        small_sums[5],
        shares[2],
        small_sums[6],
        shares[3],
    )


def solution(mesh):
    return jax.shard_map(
        per_device,
        mesh=mesh,
        in_specs=(
            P(None, None, "lat", "lon", None),
            P(None, None, "lat", "lon", None),
            P(),
            P(None, "lat", "lon"),
            P(),
            P(),
            P(),
            P(),
            P("lat", None, None),
            P(),
            P(),
            P(),
            P(),
            P(),
            P(),
            P(),
        ),
        out_specs=(
            P(None, None, "lat", "lon", None),
            P(),
            P(),
            P("lon", None),
            P(),
            P("lat", None, None),
            P("lon", None),
            P(),
            P(),
            P(),
            P("lon", None),
            P(),
            P("lon", None),
        ),
        check_vma=False,
    )
```

profile of v0, /device:TPU:2, one launch (start us, length us, event | category | flops | bytes accessed | tf_op | source)
XLA Modules:
  0.0 1616.5 jit_solution(15196454264449524395)
XLA Ops:
  12.4 12.6 collective-permute-start
  27.0 2.3 copy.237
  29.3 40.6 %gather_fusion = f32[20736,6]{1,0:T(8,128)} fusion(f32[6,6336]{0,1:T(8,128)} %bitcast.113, s32[21504]{0:T(1024)S(1)} %pad_clamp_fusion), kind=kCustom, calls=%fused_computation | custom fusion | bytes 1078272 | tf_op jit(solution)/shard_map/jvp(jit(_take))/gather | solution.py:41
  69.9 11.6 copy.238
  83.5 4.9 collective-permute-start.1
  89.0 2.6 collective-permute-done.1
  94.2 3.1 fusion.96
  97.6 2.3 fusion.34
  101.3 3.0 collective-permute-start.2
  105.0 6.4 collective-permute-done.2
  117.8 8.2 collective-permute-done.3
  133.0 2.6 fusion.32
  135.6 2.5 fusion.14
  138.2 2.3 fusion.97
  140.5 3.0 multiply_reduce_fusion.1
  149.3 3.1 collective-permute-done.4
  153.1 3.9 collective-permute-start.5
  157.1 3.0 convolution_bitcast_fusion.1
  161.9 180.7 %fusion.84 = (f32[8,192]{1,0:T(8,128)}, f32[8,768]{1,0:T(8,128)}) fusion(f32[192,192]{1,0:T(8,128)S(1)} %convolution_bitcast_fusion.5, f32[192,768]{1,0:T(8,128)} %convolution_bitcast_fusion.1), kind=kCustom, calls=%all-reduce-scatter.2 | all-reduce-scatter fusion | flops 245761 | bytes 770048
  345.5 2.7 convolution_bitcast_fusion.3
  352.7 2.7 fusion.8
  355.4 5.9 collective-permute-start.15
  365.0 3.2 convolution_bitcast_fusion.2
  368.1 6.2 copy.270
  374.3 114.3 %scatter_custom_fusion = f32[6,6336]{0,1:T(8,128)} fusion(s32[20736]{0:T(1024)} %copy-done.29, f32[20736,6]{1,0:T(8,128)} %copy.270, f32[]{:T(128)} %constant.44.clone.1), kind=kCustom, calls=%fused_computation.11 | custom fusion | flops 124416 | bytes 152576 | tf_op jit(solution)/shard_map/transpose(jvp(jit(_take)))/scatter-add | solution.py:41
  490.0 4.3 convolution_bitcast_fusion
  494.3 16.6 %collective-permute-start.13 = (f32[8,192]{1,0:T(8,128)}, f32[8,192]{1,0:T(8,128)S(1)}, u32[]{:S(2)}, u32[]{:S(2)}) collective-permute-start(f32[8,192]{1,0:T(8,128)} %get-tuple-element.117), channel_id=1, source_target_pairs={{0,6},{1,7},{2,8},{3,9},{4,10},{5,11},{6,12},{7,13},{8,14},{9,15},... | collective-permute-start | bytes 18440
  510.9 14.5 collective-permute-start.12
  527.4 2.5 copy.291
  529.8 3.0 reshape.386
  532.9 3.8 collective-permute-start.10
  536.7 2.6 collective-permute-start.9
  540.9 2.4 collective-permute-start.8
  543.4 2.8 collective-permute-start.22
  546.2 3.0 collective-permute-start.21
  549.3 2.2 collective-permute-start.20
  553.6 4.7 collective-permute-start.19
  558.2 2.8 concatenate.50
  563.2 2.5 collective-permute-start.17
  565.7 2.6 collective-permute-start.16
  568.3 3.9 collective-permute-start.6
  574.5 3.8 collective-permute-done.6
  580.3 11.6 collective-permute-done.7
  594.4 141.5 %all-reduce.8 = (f32[192]{0:T(256)}, f32[192]{0:T(256)}, f32[576]{0:T(1024)}, f32[192]{0:T(256)}, f32[192]{0:T(256)}, /*index=5*/f32[192]{0:T(256)}, f32[768]{0:T(1024)}) all-reduce(f32[192]{0:T(256)S(1)} %get-tuple-element.95, f32[192]{0:T(256)S(1)} %reduce_sum.211, ...), channel_id=1, replica_groups=mesh['lat'=16,'lon'=32] {'lat','lon'}, use_global_device_ids=true, to_apply=%region_12.13 | all-reduce | flops 2304 | bytes 18432 | tf_op jit(solution)/shard_map/psum | solution.py:181
  735.9 391.8 %all-reduce.14.cloned.1.call-done = (f32[192,576]{1,0:T(8,128)}, f32[1,6,6336]{1,2,0:T(8,128)}) async-done(((f32[192,576]{1,0:T(8,128)}, f32[1,6,6336]{1,2,0:T(8,128)}), (f32[192,576]{1,0:T(8,128)}, f32[1,6,6336]{1,2,0:T(8,128)})) %all-reduce.14.cloned.1.call-update) | async-done | bytes 594448
  1127.7 3.1 copy.275
  1131.6 387.3 %reduce-scatter.6.cloned.1.call-done = f32[24,192]{1,0:T(8,128)} async-done(((f32[768,192]{1,0:T(8,128)}), f32[24,192]{1,0:T(8,128)}) %reduce-scatter.6.cloned.1.call-update) | async-done | bytes 18448 | tf_op jit(solution)/shard_map/reduce_scatter | solution.py:179
  1519.0 90.5 %all-reduce.10 = (f32[6,576]{1,0:T(8,128)}, f32[6,192]{1,0:T(8,128)}, f32[6,768]{1,0:T(8,128)}, f32[24,192]{1,0:T(8,128)}) all-reduce(f32[6,576]{1,0:T(8,128)S(1)} %constant_dynamic-slice_fusion.2, f32[6,192]{1,0:T(8,128)S(1)} %constant_dynamic-slice_fusion.1, ...), channel_id=1, replica_groups=mesh['lat'=16,'lon'=32] {'lat'}, use_global_device_ids=true, to_apply=%region_16.17 | all-reduce | flops 13824 | bytes 110592 | tf_op jit(solution)/shard_map/psum | solution.py:174
  (251 shorter events, 61.9 us)
Async XLA Ops:
  7.2 125.8 %copy-start = (f32[192,768]{1,0:T(8,128)S(1)}, f32[192,768]{1,0:T(8,128)}, u32[]{:S(2)}) copy-start(f32[192,768]{1,0:T(8,128)} %param.29) | copy-start | bytes 1769476
  7.2 1120.4 %all-reduce.14.cloned.1.call-start = ((), (), s32[]{:S(2)}) async-start(), calls=%async_computation.2 | async-start | bytes 7471104
  11.4 13.9 copy-start.50
  11.6 15.3 copy-start.38
  12.4 70.0 %collective-permute-start = (f32[2,2,6,6,192]{4,3,2,1,0:T(8,128)}, f32[2,2,6,6,192]{4,3,2,1,0:T(8,128)}, u32[]{:S(2)}, u32[]{:S(2)}) collective-permute-start(f32[2,2,6,6,192]{4,3,2,1,0:T(8,128)} %get-tuple-element.143), channel_id=1, source_target_pairs={{32,0},{64,32},{96,64},{128,96},{160,128},{192,160},{224,192},{256... | collective-permute-start | bytes 331784 | tf_op jit(solution)/shard_map/ppermute | solution.py:16
  81.6 10.3 copy-start.8
  81.7 10.3 copy-start.53
  83.5 8.1 collective-permute-start.1
  100.9 13.4 copy-start.4
  101.3 10.1 collective-permute-start.2
  112.1 13.9 collective-permute-start.3
  146.8 10.3 copy-start.20
  146.8 10.3 copy-start.26
  146.8 10.3 copy-start.34
  146.8 10.3 copy-start.59
  146.8 10.3 copy-start.64
  147.3 5.2 collective-permute-start.4
  153.1 7.6 collective-permute-start.5
  161.4 184.1 %copy-start.41 = (f32[2,6,144]{2,1,0:T(8,128)S(1)}, f32[2,6,144]{2,1,0:T(8,128)}, u32[]{:S(2)}) copy-start(f32[2,6,144]{2,1,0:T(8,128)} %copy-done.39) | copy-start | bytes 20740
  343.3 193.4 %collective-permute-start.14 = (f32[8,192]{1,0:T(8,128)}, f32[8,192]{1,0:T(8,128)S(1)}, u32[]{:S(2)}, u32[]{:S(2)}) collective-permute-start(f32[8,192]{1,0:T(8,128)} %get-tuple-element.117), channel_id=1, source_target_pairs={{0,7},{1,8},{2,9},{3,10},{4,11},{5,12},{6,13},{7,14},{8,15},{9,16}... | collective-permute-start | bytes 18440
  355.4 177.5 %collective-permute-start.15 = (f32[6,192]{1,0:T(8,128)S(1)}, f32[6,192]{1,0:T(8,128)S(1)}, u32[]{:S(2)}, u32[]{:S(2)}) collective-permute-start(f32[6,192]{1,0:T(8,128)S(1)} %slice.149), channel_id=1, source_target_pairs={{0,8},{1,9},{2,10},{3,11},{4,12},{5,13},{6,14},{7,15},{8,16},{9,17... | collective-permute-start | bytes 13832
  488.7 1030.3 %reduce-scatter.6.cloned.1.call-start = ((), (), s32[]{:S(2)}) async-start(), calls=%async_computation.1 | async-start | bytes 811008 | tf_op jit(solution)/shard_map/reduce_scatter | solution.py:179
  494.3 46.6 %collective-permute-start.13 = (f32[8,192]{1,0:T(8,128)}, f32[8,192]{1,0:T(8,128)S(1)}, u32[]{:S(2)}, u32[]{:S(2)}) collective-permute-start(f32[8,192]{1,0:T(8,128)} %get-tuple-element.117), channel_id=1, source_target_pairs={{0,6},{1,7},{2,8},{3,9},{4,10},{5,11},{6,12},{7,13},{8,14},{9,15},... | collective-permute-start | bytes 18440
  510.9 32.4 %collective-permute-start.12 = (f32[8,192]{1,0:T(8,128)}, f32[8,192]{1,0:T(8,128)S(1)}, u32[]{:S(2)}, u32[]{:S(2)}) collective-permute-start(f32[8,192]{1,0:T(8,128)} %get-tuple-element.117), channel_id=1, source_target_pairs={{0,5},{1,6},{2,7},{3,8},{4,9},{5,10},{6,11},{7,12},{8,13},{9,14},{... | collective-permute-start | bytes 18440
  525.4 20.8 %collective-permute-start.11 = (f32[8,192]{1,0:T(8,128)}, f32[8,192]{1,0:T(8,128)S(1)}, u32[]{:S(2)}, u32[]{:S(2)}) collective-permute-start(f32[8,192]{1,0:T(8,128)} %get-tuple-element.117), channel_id=1, source_target_pairs={{0,4},{1,5},{2,6},{3,7},{4,8},{5,9},{6,10},{7,11},{8,12},{9,13},{1... | collective-permute-start | bytes 18440
  529.8 9.5 copy-start.9
  532.9 20.6 %copy-start.23 = (f32[2,2,12,3,192]{4,3,2,1,0:T(4,128)S(1)}, f32[2,2,12,3,192]{4,3,2,1,0:T(4,128)}, u32[]{:S(2)}) copy-start(f32[2,2,12,3,192]{4,3,2,1,0:T(4,128)} %copy-done.22) | copy-start | bytes 331780
  532.9 20.7 %copy-start.54 = (f32[192]{0:T(256)S(1)}, f32[192]{0:T(256)}, u32[]{:S(2)}) copy-start(f32[192]{0:T(256)} %get-tuple-element.121) | copy-start | bytes 2308
  532.9 18.6 %copy-start.49 = (f32[6,192]{1,0:T(8,128)}, f32[6,192]{1,0:T(8,128)S(1)}, u32[]{:S(2)}) copy-start(f32[6,192]{1,0:T(8,128)S(1)} %collective-permute-done.15) | copy-start | bytes 13828
  532.9 16.4 %collective-permute-start.10 = (f32[8,192]{1,0:T(8,128)}, f32[8,192]{1,0:T(8,128)S(1)}, u32[]{:S(2)}, u32[]{:S(2)}) collective-permute-start(f32[8,192]{1,0:T(8,128)} %get-tuple-element.117), channel_id=1, source_target_pairs={{0,3},{1,4},{2,5},{3,6},{4,7},{5,8},{6,9},{7,10},{8,11},{9,12},{10... | collective-permute-start | bytes 18440
  536.7 14.7 copy-start.48
  536.7 14.7 collective-permute-start.9
  540.9 12.6 collective-permute-start.8
  543.4 19.8 %collective-permute-start.22 = (f32[8,768]{1,0:T(8,128)S(1)}, f32[8,768]{1,0:T(8,128)S(1)}, u32[]{:S(2)}, u32[]{:S(2)}) collective-permute-start(f32[8,768]{1,0:T(8,128)S(1)} %copy-done.37), channel_id=1, source_target_pairs={{0,7},{1,8},{2,9},{3,10},{4,11},{5,12},{6,13},{7,14},{8,15},{9,16}... | collective-permute-start | bytes 73736
  546.2 19.5 %collective-permute-start.21 = (f32[8,768]{1,0:T(8,128)S(1)}, f32[8,768]{1,0:T(8,128)S(1)}, u32[]{:S(2)}, u32[]{:S(2)}) collective-permute-start(f32[8,768]{1,0:T(8,128)S(1)} %copy-done.37), channel_id=1, source_target_pairs={{0,6},{1,7},{2,8},{3,9},{4,10},{5,11},{6,12},{7,13},{8,14},{9,15},... | collective-permute-start | bytes 73736
  549.3 19.0 %collective-permute-start.20 = (f32[8,768]{1,0:T(8,128)S(1)}, f32[8,768]{1,0:T(8,128)S(1)}, u32[]{:S(2)}, u32[]{:S(2)}) collective-permute-start(f32[8,768]{1,0:T(8,128)S(1)} %copy-done.37), channel_id=1, source_target_pairs={{0,5},{1,6},{2,7},{3,8},{4,9},{5,10},{6,11},{7,12},{8,13},{9,14},{... | collective-permute-start | bytes 73736
  551.5 9.6 collective-permute-start.23
  553.6 18.7 %collective-permute-start.19 = (f32[8,768]{1,0:T(8,128)S(1)}, f32[8,768]{1,0:T(8,128)S(1)}, u32[]{:S(2)}, u32[]{:S(2)}) collective-permute-start(f32[8,768]{1,0:T(8,128)S(1)} %copy-done.37), channel_id=1, source_target_pairs={{0,4},{1,5},{2,6},{3,7},{4,8},{5,9},{6,10},{7,11},{8,12},{9,13},{1... | collective-permute-start | bytes 73736
  561.0 11.2 collective-permute-start.18
  563.2 9.1 collective-permute-start.17
  565.7 7.9 collective-permute-start.16
  568.3 10.0 collective-permute-start.6
  578.3 13.8 copy-start.15
  578.3 13.8 copy-start.46
  578.4 13.6 collective-permute-start.7
  580.3 12.2 copy-start.44
  580.3 12.3 copy-start.28
  1127.7 481.8 %copy-start.1 = (f32[192,768]{1,0:T(8,128)S(1)}, f32[192,768]{1,0:T(8,128)}, u32[]{:S(2)}) copy-start(f32[192,768]{1,0:T(8,128)} %param.29) | copy-start | bytes 1769476
  (43 other events, 104.6 us)
Sparse Core Ops, SparseCore 0:
  488.8 638.8 all-reduce.13
  1134.8 384.0 reduce-scatter.5
where the time goes:
time: 1640 us; the launch traced here: 1620 us
  waiting for transfers between devices  817 us (50%)
  blocking collectives  413 us (25%)
  other arithmetic  135 us (8%)
  starting transfers between devices  106 us (6%)
  local copies, waits for them, and re-layouts  92.3 us (6%)
  matrix products  37.3 us (2%)
  between operations  17 us (1%)
    unnamed x19, waiting for transfers between devices  393 us
    reduce_scatter x1, waiting for transfers between devices, per_device(): lax.psum_scatter(totals[3], 'lon', scatter_dimension=0, tiled=True)  387 us
    unnamed x1, blocking collectives  181 us
    psum x1, blocking collectives, per_device(): lax.psum((norm1_grads[0], norm1_grads[1], attend_grads[1], attend_grads[4...  141 us
    scatter-add x1, other arithmetic, position_bias(): picked = jnp.take(table_rows, position.reshape(-1), axis=-1)  114 us
    psum x1, blocking collectives, per_device(): lax.psum((large_grads[0], large_grads[1], large_grads[2], large_grads[3])...  90.5 us
    unnamed x17, starting transfers between devices  71.1 us
    gather x2, local copies, waits for them, and re-layouts, position_bias(): picked = jnp.take(table_rows, position.reshape(-1), axis=-1)  52.2 us
  transfers between devices with their start and end apart: 26, of which 10 were waited for; matrix products, arithmetic and copies ran while one was open for 14% of the time, Pallas kernels for 0%

commit v1 on v0

v1 whole, which is shorter than its diff:
```python
import functools
import math

import jax
import jax.numpy as jnp
import numpy as np
from jax import lax
from jax.experimental import pallas as pl
from jax.experimental.pallas import tpu as pltpu
from jax.sharding import PartitionSpec as P

f32 = jnp.float32
bf16 = jnp.bfloat16
MESH = pl.DeviceIdType.MESH
C = 192
HEADS = 6
HID = 768
TOK = 144
ZH = 24
REL = 11
FLAT = 132
eps = 1e-05
kept = 1.25
scale = 1.0 / math.sqrt(32.0)
VMEM_LIMIT = 56 * 1024 * 1024


def bias_order():
    to = np.zeros((384, 384), np.float32)
    rest = np.zeros((384, 128), np.float32)
    for z in range(2):
        for h in range(12):
            for r in range(REL):
                lane = z * FLAT + h * REL + r
                spot = (REL - 1 - r) * ZH + (h // 6) * 12 + z * 6 + h % 6
                to[lane, spot] = 1.0
                if lane >= 256:
                    for head in range(HEADS):
                        rest[spot, 8 * head + lane - 256] = 1.0
    return to, rest


def spread_order():
    to = np.zeros((C, 256), np.float32)
    for feature in range(C):
        to[feature, 8 * (feature // 6) + feature % 6] = 1.0
    return to


def halves(values):
    high = values.astype(bf16)
    return high, (values - high.astype(f32)).astype(bf16)


def thirds(values):
    high = values.astype(bf16)
    left = values - high.astype(f32)
    mid = left.astype(bf16)
    return high, mid, (left - mid.astype(f32)).astype(bf16)


def one(a, b, ca, cb):
    return lax.dot_general(a, b, (((ca,), (cb,)), ((), ())), preferred_element_type=f32)


def product(a, b, ca=1, cb=0):
    return one(a[0], b[0], ca, cb) + (one(a[0], b[1], ca, cb) + one(a[1], b[0], ca, cb))


def norm_parts(values):
    center = values - jnp.mean(values, axis=-1, keepdims=True)
    spread = jnp.mean(center * center, axis=-1, keepdims=True)
    inv = lax.rsqrt(spread + eps)
    return center * inv, inv


def norm_back(grad, gain, unit, inv):
    scaled = grad * gain
    return inv * (
        scaled
        - jnp.mean(scaled, axis=-1, keepdims=True)
        - unit * jnp.mean(scaled * unit, axis=-1, keepdims=True)
    )


def token_row(hh, wh, w3):
    return (wh * 3 + w3) * ZH + hh * 12


def neighbour(lat, lon, lats, lons, dlat, dlon):
    return lax.rem(lat + dlat + lats, lats), lax.rem(lon + dlon + lons, lons)


def halo_kernel(lats, lons, keep, fields, cot, win, loc, out_buf, in_buf, send_sem, recv_sem):
    lat = lax.axis_index("lat")
    lon = lax.axis_index("lon")
    at = functools.partial(neighbour, lat, lon, lats, lons)
    barrier = pltpu.get_barrier_semaphore()
    for dlat, dlon in ((1, 0), (0, 1), (1, 1)):
        pl.semaphore_signal(barrier, inc=1, device_id=at(dlat, dlon), device_id_type=MESH)
    attn = 1 - keep[0, 0]

    def rows(sample, sh, sw, w3, zz):
        part = (sample, 1 - zz, pl.ds(sh * 6, 6), sw * 3 + w3, slice(None))
        return jnp.concatenate([fields[part], cot[part]], axis=-1)

    copies = []
    for slot, (sh, sw) in enumerate(((0, 0), (0, 1), (1, 0))):
        for w3 in range(3):
            for zz in range(2):
                out_buf[slot, pl.ds(w3 * 12 + zz * 6, 6), :] = rows(attn, sh, sw, w3, zz)
        if slot == 0:
            pl.semaphore_wait(barrier, 3)
        copy = pltpu.make_async_remote_copy(
            src_ref=out_buf.at[slot],
            dst_ref=in_buf.at[slot],
            send_sem=send_sem.at[slot],
            recv_sem=recv_sem.at[slot],
            device_id=at(-1 if sh == 0 else 0, -1 if sw == 0 else 0),
            device_id_type=MESH,
        )
        copy.start()
        copies.append(copy)
    for w3 in range(3):
        for zz in range(2):
            win[pl.ds(token_row(0, 0, w3) + zz * 6, 6), :] = rows(attn, 1, 1, w3, zz)
            for sh in range(2):
                for sw in range(2):
                    start = token_row(1 - sh, 1 - sw, w3) + zz * 6
                    loc[pl.ds(start, 6), :] = rows(1 - attn, sh, sw, w3, zz)
    for slot, (sh, sw) in enumerate(((0, 0), (0, 1), (1, 0))):
        copies[slot].wait_recv()
        for w3 in range(3):
            start = token_row(1 - sh, 1 - sw, w3)
            win[pl.ds(start, 12), :] = in_buf[slot, pl.ds(w3 * 12, 12), :]
    for copy in copies:
        copy.wait_send()


def compute_kernel(
    keep, win, loc, region, n1g, n1s, wqkv, bqkv, table, wproj, bproj, n2g, n2s, win_w, b_in, wout,
    order, rest, spread,
    large, tabs, dxa, other,
    tab_in, bias_s, attn_s, diff_s, qp_s, mi_s, mo_s, row_s, tab_s,
):
    x = win[:, 0:C]
    cot = win[:, C : 2 * C]
    unit1, inv1 = norm_parts(x)
    gain1 = n1g[...].reshape(1, C)
    normed1 = halves(unit1 * gain1 + n1s[...].reshape(1, C))
    w_qkv = halves(wqkv[...])
    proj = product(normed1, w_qkv) + bqkv[...].reshape(1, 3 * C)
    query = halves(proj[:, 0:C] * scale)
    key = halves(proj[:, C : 2 * C])
    value = halves(proj[:, 2 * C : 3 * C])

    tab_in[...] = jnp.zeros(tab_in.shape, f32)
    for zn in range(2):
        for hn in range(12):
            spot = (hn // 6) * 12 + zn * 6 + hn % 6
            for zm in range(2):
                start = ((zn * 2 + zm) * 12 + hn) * FLAT
                tab_in[pl.ds(spot * 8, HEADS), zm * FLAT : (zm + 1) * FLAT] = table[0, :, start : start + FLAT]
    shifted = None
    for part in thirds(tab_in[...]):
        term = one(part, order[...], 1, 0)
        shifted = term if shifted is None else shifted + term
    for l in range(3):
        bias_s[l] = shifted[:, l * 128 : l * 128 + 128]

    marks = region[...].astype(f32)
    columns = []
    for w in range(6):
        for hh in range(2):
            for z in range(2):
                columns.append(jnp.broadcast_to(marks[z, hh * 6 : hh * 6 + 6, w : w + 1], (6, TOK)))
    mark_rows = jnp.concatenate(columns, axis=0)
    same = mark_rows == mark_rows.T

    lanes = lax.broadcasted_iota(jnp.int32, (1, C), 1)
    masks = [(lanes // 32 == h) for h in range(HEADS)]

    def masked(pair, h):
        zero = jnp.zeros((), bf16)
        return tuple(jnp.where(masks[h], part, zero) for part in pair)

    mixed = jnp.zeros((TOK, C), f32)
    for h in range(HEADS):
        scores = product(masked(query, h), key, 1, 1)
        strip = jnp.concatenate([bias_s[l, pl.ds(h, ZH, stride=8), :] for l in range(3)], axis=1)
        bias = jnp.concatenate(
            [pltpu.roll(strip, (384 - (5 - wn) * ZH) % 384, axis=1)[:, 0:TOK] for wn in range(6)], axis=0
        )
        scores = jnp.where(same, scores + bias, -1e30)
        scores = jnp.exp(scores - jnp.max(scores, axis=-1, keepdims=True))
        attn = scores / jnp.sum(scores, axis=-1, keepdims=True)
        attn_s[h] = attn
        mixed = mixed + product(halves(attn), masked(value, h))
    mixed = halves(mixed)
    w_proj = halves(wproj[...])
    branch = product(mixed, w_proj) + bproj[...].reshape(1, C)

    both = keep[0, 0] == keep[0, 1]
    loc_x = loc[:, 0:C]
    loc_cot = loc[:, C : 2 * C]
    middle = jnp.where(both, x + kept * branch, loc_x)
    cot_m = jnp.where(both, cot, loc_cot)
    unit2, inv2 = norm_parts(middle)
    gain2 = n2g[...].reshape(1, C)
    normed2 = halves(unit2 * gain2 + n2s[...].reshape(1, C))
    w_in = halves(win_w[...])
    hidden = product(normed2, w_in) + b_in[...].reshape(1, HID)
    cdf = 0.5 * (1.0 + lax.erf(hidden * math.sqrt(0.5)))
    slope = cdf + hidden * jnp.exp(-0.5 * hidden * hidden) * (1.0 / math.sqrt(2.0 * math.pi))
    grad_y = halves(kept * cot_m)
    w_out = halves(wout[...])
    grad_hidden = halves(product(grad_y, w_out, 1, 1) * slope)
    mo_s[:, 0:C] = product(halves(hidden * cdf), grad_y, 0, 0)

    ones_lane = (lax.broadcasted_iota(jnp.int32, (1, 256), 1) & 7) == 6

    def spread_out(pair):
        high = one(pair[0], spread[...], 1, 0)
        low = one(pair[1], spread[...], 1, 0)
        return jnp.where(ones_lane, 1.0, high).astype(bf16), low.astype(bf16)

    mi_s[...] = product(spread_out(normed2), grad_hidden, 0, 0)
    grad_n2 = product(grad_hidden, w_in, 1, 1)
    row_s[0:1, 2 * C : 3 * C] = jnp.sum(grad_n2 * unit2, axis=0, keepdims=True)
    row_s[0:1, 3 * C : 4 * C] = jnp.sum(grad_n2, axis=0, keepdims=True)
    grad_m = cot_m + norm_back(grad_n2, gain2, unit2, inv2)
    grad_a = jnp.where(both, grad_m, cot)
    other[...] = jnp.where(both, loc_cot, grad_m)

    grad_b = halves(kept * grad_a)
    qp_s[:, 3 * C : 4 * C] = product(spread_out(mixed), grad_b, 0, 0)
    grad_o = halves(product(grad_b, w_proj, 1, 1))
    grad_q = jnp.zeros((TOK, C), f32)
    grad_k = jnp.zeros((TOK, C), f32)
    grad_v = jnp.zeros((TOK, C), f32)
    diff_s[...] = jnp.zeros(diff_s.shape, f32)
    for h in range(HEADS):
        attn = attn_s[h]
        grad_oh = masked(grad_o, h)
        grad_attn = product(grad_oh, value, 1, 1)
        grad_v = grad_v + product(halves(attn), grad_oh, 0, 0)
        term = attn * grad_attn
        grad_s = term - attn * jnp.sum(term, axis=-1, keepdims=True)
        grad_sp = halves(grad_s)
        grad_q = grad_q + product(grad_sp, masked(key, h))
        grad_k = grad_k + product(grad_sp, masked(query, h), 0, 0)
        wide = jnp.concatenate([grad_s, jnp.zeros((TOK, 384 - TOK), f32)], axis=1)
        total = None
        for wn in range(6):
            block = wide[wn * ZH : (wn + 1) * ZH, :]
            if wn < 5:
                block = pltpu.roll(block, (5 - wn) * ZH, axis=1)
            total = block if total is None else total + block
        for l in range(3):
            diff_s[l, pl.ds(h, ZH, stride=8), :] = total[:, l * 128 : l * 128 + 128]
    grad_p = halves(jnp.concatenate([grad_q * scale, grad_k, grad_v], axis=1))
    qp_s[:, 0 : 3 * C] = product(spread_out(normed1), grad_p, 0, 0)
    grad_n1 = product(grad_p, w_qkv, 1, 1)
    row_s[0:1, 0:C] = jnp.sum(grad_n1 * unit1, axis=0, keepdims=True)
    row_s[0:1, C : 2 * C] = jnp.sum(grad_n1, axis=0, keepdims=True)
    grad_x = grad_a + norm_back(grad_n1, gain1, unit1, inv1)
    for hh in range(2):
        for wh in range(2):
            for w3 in range(3):
                start = token_row(hh, wh, w3)
                dxa[hh * 2 + wh, pl.ds(w3 * 12, 12), :] = grad_x[start : start + 12, :]

    diff = halves(jnp.concatenate([diff_s[l] for l in range(3)], axis=1))
    back = one(diff[0], order[...], 1, 1) + one(diff[1], order[...], 1, 1)
    tail = one(diff[0], rest[...], 1, 0) + one(diff[1], rest[...], 1, 0)
    row_id = lax.broadcasted_iota(jnp.int32, tail.shape, 0) & 7
    lane_id = lax.broadcasted_iota(jnp.int32, tail.shape, 1) // 8
    tail = jnp.where(row_id == lane_id, tail, 0.0).reshape(ZH, 8, 128).sum(axis=1)
    for l in range(2):
        tab_s[l] = back[:, l * 128 : l * 128 + 128]
    tab_s[0, pl.ds(6, ZH, stride=8), :] = tail
    for k in range(8):
        for l in range(2):
            tabs[2 * k + l] = tab_s[l, 24 * k : 24 * k + 24, :]

    mi_rows = lax.broadcasted_iota(jnp.int32, (256, 1), 0) & 7
    mi_s[...] = jnp.where(mi_rows == 7, row_s[0:1, :], mi_s[...])
    low_lanes = lax.broadcasted_iota(jnp.int32, (8, 128), 1) < 64

    def pack(j, carry):
        a = lax.rem(j // 4, 4)
        b = lax.rem(j, 4)
        zh = j // 16
        at8 = pl.ds(pl.multiple_of(j * 8, 8), 8)

        def put(piece, tile, rows=slice(None)):
            if piece < 8:
                large[0, a, b, zh, piece, rows, :] = tile
            else:
                large[1, b, a, zh, piece - 8, rows, :] = tile

        for piece in range(6):
            put(piece, qp_s[at8, piece * 128 : piece * 128 + 128])
            put(piece + 6, mi_s[at8, piece * 128 : piece * 128 + 128])
        tails = []
        for k in range(3):
            at = pl.ds(pl.multiple_of(j * 24 + k * 8, 8), 8)
            put(12 + k, mo_s[at, 0:128])
            tails.append(mo_s[at, 128:256])
        put(15, jnp.where(low_lanes, tails[0], pltpu.roll(tails[1], 64, axis=1)))
        pairs = jnp.where(low_lanes, tails[2], pltpu.roll(pltpu.roll(tails[2], 64, axis=1), 7, axis=0))
        for k in range(4):
            put(k, pairs[2 * k : 2 * k + 1, :], slice(7, 8))
        return carry

    lax.fori_loop(0, 32, pack, 0)


def sums_kernel(
    lats, lons, keep, large, tabs, dxa, other,
    fields_grad, n1g_o, n1s_o, qkvw_o, qkvb_o, table_o, projw_o, projb_o, n2g_o, n2s_o, inw_o, inb_o, outw_o,
    back_in, pair_in, a_in, b_in, z_in, gather, tab_in, tab_pair, tab_sum, tab_all, acc_a, acc_b, mine, wide_s,
    back_ss, back_rs, pair_ss, pair_rs, a_ss, a_rs, b_ss, b_rs, z_ss, z_rs, g_ss, g_rs, t_ss, t_rs, tp_ss, tp_rs, tg_ss, tg_rs,
):
    lat = lax.axis_index("lat")
    lon = lax.axis_index("lon")
    core = lax.rem(lat, 2)
    zl = lat // 2
    zh = lon // 16
    plane = lax.rem(lon, 16)
    px = plane // 4
    py = lax.rem(plane, 4)
    at = functools.partial(neighbour, lat, lon, lats, lons)

    barrier = pltpu.get_barrier_semaphore()

    def hello(device):
        pl.semaphore_signal(barrier, inc=1, device_id=device, device_id_type=MESH)

    for dlat, dlon in ((-1, 0), (0, -1), (-1, -1)):
        hello(at(dlat, dlon))
    for d in range(1, 16):
        hello((lax.rem(lat + d, 16), lon))
        hello((lat, zh * 16 + lax.rem(plane + d, 16)))
    for d in range(8):
        hello((lax.rem(lat + 2 * d, 16), lax.rem(lon + 16, 32)))
    pl.semaphore_wait(barrier, 3 + 30 + 8)

    def send(src, dst, ss, rs, device):
        copy = pltpu.make_async_remote_copy(
            src_ref=src, dst_ref=dst, send_sem=ss, recv_sem=rs, device_id=device, device_id_type=MESH
        )
        copy.start()
        return copy

    every = []

    pair = send(large.at[1 - core], pair_in, pair_ss, pair_rs, (lat + 1 - 2 * core, lon))
    every.append(pair)
    home = []
    for slot, (hh, wh) in enumerate(((1, 1), (1, 0), (0, 1))):
        home.append(send(dxa.at[hh * 2 + wh], back_in.at[slot], back_ss.at[slot], back_rs.at[slot], at(hh, wh)))
    every += home
    tab_copies = []
    for d in range(1, 16):
        to = lax.rem(plane + d, 16)
        tab_copies.append(
            send(tabs.at[to], tab_in.at[d - 1], t_ss.at[d - 1], t_rs.at[d - 1], (lat, zh * 16 + to))
        )
    every += tab_copies

    pair.wait_recv()

    def add_pair(i, carry):
        for j in range(4):
            pair_in[i, j] = pair_in[i, j] + large[core, i, j]
        return carry

    lax.fori_loop(0, 4, add_pair, 0)
    first = px + core * (py - px)
    second = py + core * (px - py)

    def along(pos_first, pos_second):
        x = pos_first + core * (pos_second - pos_first)
        y = pos_second + core * (pos_first - pos_second)
        return lat, zh * 16 + x * 4 + y

    a_copies = []
    for d in range(1, 4):
        to = lax.rem(first + d, 4)
        a_copies.append(
            send(pair_in.at[to], a_in.at[d - 1], a_ss.at[d - 1], a_rs.at[d - 1], along(to, second))
        )
    every += a_copies

    for copy in tab_copies:
        copy.wait_recv()
    total = tabs[plane]
    for d in range(15):
        total = total + tab_in[d]
    tab_sum[...] = total
    tab_across = send(tab_sum, tab_pair, tp_ss, tp_rs, (lat, lax.rem(lon + 16, 32)))
    every.append(tab_across)

    for copy in a_copies:
        copy.wait_recv()
    for j in range(4):
        acc_a[j] = (pair_in[first, j] + a_in[0, j]) + (a_in[1, j] + a_in[2, j])
    b_copies = []
    for d in range(1, 4):
        to = lax.rem(second + d, 4)
        b_copies.append(send(acc_a.at[to], b_in.at[d - 1], b_ss.at[d - 1], b_rs.at[d - 1], along(first, to)))
    every += b_copies

    tab_across.wait_recv()
    tab_all[plane] = tab_sum[...] + tab_pair[...]
    tab_back = []
    for d in range(1, 16):
        to = lax.rem(plane + d, 16)
        tab_back.append(
            send(tab_all.at[plane], tab_all.at[plane], tg_ss.at[d - 1], tg_rs.at[d - 1], (lat, zh * 16 + to))
        )
    every += tab_back

    for copy in b_copies:
        copy.wait_recv()
    acc_b[...] = (acc_a[second] + b_in[0]) + (b_in[1] + b_in[2])
    z_copies = []
    for d in range(1, 16):
        to = lax.rem(zh * 8 + zl + d, 16)
        z_copies.append(
            send(
                acc_b.at[to // 8, lax.rem(to, 8)], z_in.at[d - 1], z_ss.at[d - 1], z_rs.at[d - 1],
                (lax.rem(to, 8) * 2 + core, (to // 8) * 16 + plane),
            )
        )
    every += z_copies

    for copy in home:
        copy.wait_recv()
    first_kept = keep[0, 0] == 1
    for sh in range(2):
        for sw in range(2):
            for w3 in range(3):
                if (sh, sw) == (1, 1):
                    from_a = dxa[0, pl.ds(w3 * 12, 12), :]
                else:
                    from_a = back_in[sh * 2 + sw, pl.ds(w3 * 12, 12), :]
                from_o = other[pl.ds(token_row(1 - sh, 1 - sw, w3), 12), :]
                tops = (jnp.where(first_kept, from_a, from_o), jnp.where(first_kept, from_o, from_a))
                for sample in range(2):
                    for zz in range(2):
                        fields_grad[sample, 1 - zz, pl.ds(sh * 6, 6), sw * 3 + w3, :] = tops[sample][
                            zz * 6 : zz * 6 + 6, :
                        ]

    for copy in z_copies:
        copy.wait_recv()
    total = acc_b[zh, zl]
    for d in range(15):
        total = total + z_in[d]
    slot = core * 8 + zl
    gather[slot] = total
    mine[...] = total
    g_copies = []
    for d in range(1, 16):
        to = lax.rem(lat + d, 16)
        g_copies.append(send(mine, gather.at[slot], g_ss.at[d - 1], g_rs.at[d - 1], (to, lon)))
    every += g_copies

    for copy in tab_back:
        copy.wait_recv()
    for k in range(8):
        for l in range(2):
            wide_s[l, 24 * k : 24 * k + 24, :] = tab_all[2 * k + l]
    tail = wide_s[0, pl.ds(6, ZH, stride=8), :]
    for h in range(HEADS):
        moved = tail if h == 0 else pltpu.roll(tail, 128 - 8 * h, axis=1)
        wide_s[2, pl.ds(h, ZH, stride=8), :] = moved
    for zn in range(2):
        for hn in range(12):
            spot = (hn // 6) * 12 + zn * 6 + hn % 6
            block = jnp.concatenate([wide_s[l, spot * 8 : spot * 8 + 8, :] for l in range(3)], axis=1)
            for zm in range(2):
                start = ((zn * 2 + zm) * 12 + hn) * FLAT
                table_o[0, :, start : start + FLAT] = block[0:HEADS, zm * FLAT : (zm + 1) * FLAT]

    for copy in g_copies:
        copy.wait_recv()

    def strip(first_piece, count, row, rows):
        return jnp.concatenate([gather[p, row : row + rows, :] for p in range(first_piece, first_piece + count)], axis=1)

    sums = strip(0, 6, 0, 6)
    qkvw_o[...] = sums[:, 0 : 3 * C]
    projw_o[...] = sums[:, 3 * C : 4 * C]
    inw_o[...] = strip(6, 6, 0, 6)
    small = strip(0, 6, 6, 1)
    qkvb_o[...] = small[:, 0 : 3 * C].reshape(3 * C)
    projb_o[...] = small[:, 3 * C : 4 * C].reshape(C)
    inb_o[...] = strip(6, 6, 6, 1).reshape(HID)
    norms = strip(6, 6, 7, 1)
    for i, ref in enumerate((n1g_o, n1s_o, n2g_o, n2s_o)):
        ref[...] = norms[:, i * C : (i + 1) * C].reshape(C)
    for k in range(3):
        outw_o[8 * k : 8 * k + 8, 0:128] = gather[12 + k]
    outw_o[0:8, 128:192] = gather[15, :, 0:64]
    outw_o[8:16, 128:192] = pltpu.roll(gather[15], 64, axis=1)[:, 0:64]
    for k in range(4):
        line = gather[k, 7:8, :]
        outw_o[16 + 2 * k : 17 + 2 * k, 128:192] = line[:, 0:64]
        outw_o[17 + 2 * k : 18 + 2 * k, 128:192] = pltpu.roll(line, 64, axis=1)[:, 0:64]
    for copy in every:
        copy.wait_send()


def shape(*dims):
    return jax.ShapeDtypeStruct(dims, f32)


def vmem():
    return pl.BlockSpec(memory_space=pltpu.VMEM)


def smem():
    return pl.BlockSpec(memory_space=pltpu.SMEM)


def per_device(lats, lons, fields, cotangent, keep_mask, region_ids, *weights):
    order, rest = (jnp.asarray(m, bf16) for m in bias_order())
    spread = jnp.asarray(spread_order(), bf16)
    dma = pltpu.SemaphoreType.DMA
    win, loc = pl.pallas_call(
        functools.partial(halo_kernel, lats, lons),
        out_shape=(shape(TOK, 2 * C), shape(TOK, 2 * C)),
        in_specs=[smem(), vmem(), vmem()],
        out_specs=(vmem(), vmem()),
        scratch_shapes=[
            pltpu.VMEM((3, 36, 2 * C), f32),
            pltpu.VMEM((3, 36, 2 * C), f32),
            dma((3,)),
            dma((3,)),
        ],
        compiler_params=pltpu.CompilerParams(collective_id=0, has_side_effects=True, vmem_limit_bytes=VMEM_LIMIT),
        name="halo_in",
    )(keep_mask, fields, cotangent)
    large, tabs, dxa, other = pl.pallas_call(
        compute_kernel,
        out_shape=(shape(2, 4, 4, 2, 8, 8, 128), shape(16, 24, 128), shape(4, 36, C), shape(TOK, C)),
        in_specs=[smem()] + [vmem()] * 18,
        out_specs=(vmem(),) * 4,
        scratch_shapes=[
            pltpu.VMEM((192, 384), f32),
            pltpu.VMEM((3, 192, 128), f32),
            pltpu.VMEM((HEADS, TOK, TOK), f32),
            pltpu.VMEM((3, 192, 128), f32),
            pltpu.VMEM((256, 768), f32),
            pltpu.VMEM((256, 768), f32),
            pltpu.VMEM((768, 256), f32),
            pltpu.VMEM((8, 768), f32),
            pltpu.VMEM((2, 192, 128), f32),
        ],
        compiler_params=pltpu.CompilerParams(vmem_limit_bytes=VMEM_LIMIT),
        name="block_both_ways",
    )(keep_mask, win, loc, region_ids, *weights, order, rest, spread)
    tile = (8, 128)
    return pl.pallas_call(
        functools.partial(sums_kernel, lats, lons),
        out_shape=(
            shape(2, 2, 12, 6, C), shape(C), shape(C), shape(6, 3 * C), shape(3 * C), shape(1, HEADS, 6336),
            shape(6, C), shape(C), shape(C), shape(C), shape(6, HID), shape(HID), shape(24, C),
        ),
        in_specs=[smem()] + [vmem()] * 4,
        out_specs=(vmem(),) * 13,
        scratch_shapes=[
            pltpu.VMEM((3, 36, C), f32),
            pltpu.VMEM((4, 4, 2, 8) + tile, f32),
            pltpu.VMEM((3, 4, 2, 8) + tile, f32),
            pltpu.VMEM((3, 2, 8) + tile, f32),
            pltpu.VMEM((15,) + tile, f32),
            pltpu.VMEM((16,) + tile, f32),
            pltpu.VMEM((15, 24, 128), f32),
            pltpu.VMEM((24, 128), f32),
            pltpu.VMEM((24, 128), f32),
            pltpu.VMEM((16, 24, 128), f32),
            pltpu.VMEM((4, 2, 8) + tile, f32),
            pltpu.VMEM((2, 8) + tile, f32),
            pltpu.VMEM(tile, f32),
            pltpu.VMEM((3, 192, 128), f32),
            dma((3,)), dma((3,)), dma, dma, dma((3,)), dma((3,)), dma((3,)), dma((3,)),
            dma((15,)), dma((15,)), dma((15,)), dma((15,)), dma((15,)), dma((15,)), dma, dma, dma((15,)), dma((15,)),
        ],
        compiler_params=pltpu.CompilerParams(collective_id=1, has_side_effects=True, vmem_limit_bytes=VMEM_LIMIT),
        name="gradient_sums",
    )(keep_mask, large, tabs, dxa, other)


def solution(mesh):
    grid = P(None, None, "lat", "lon", None)
    rows = P("lon", None)
    return jax.shard_map(
        functools.partial(per_device, mesh.shape["lat"], mesh.shape["lon"]),
        mesh=mesh,
        in_specs=(grid, grid, P(), P(None, "lat", "lon"), P(), P(), P(), P(), P("lat", None, None))
        + (P(),) * 7,
        out_specs=(grid, P(), P(), rows, P(), P("lat", None, None), rows, P(), P(), P(), rows, P(), rows),
        check_vma=False,
    )
```

time: 1640 us -> 124 us (0.08)
  the two profiles are of different devices: /device:TPU:2 before, /device:TPU:1 now
where the time goes in v1:
time: 124 us; the launch traced here: 123 us
  Pallas kernels  97.3 us (78%)
  local copies, waits for them, and re-layouts  25.3 us (20%)
    pallas_call x1, Pallas kernels, per_device(): pl.pallas_call(functools.partial(sums_kernel, lats, lons), out_shape=(sha...  48.9 us
    pallas_call x1, Pallas kernels, per_device(): pl.pallas_call(functools.partial(halo_kernel, lats, lons), out_shape=(sha...  33.6 us
    unnamed x18, local copies, waits for them, and re-layouts  21.6 us
    pallas_call x1, Pallas kernels, per_device(): pl.pallas_call(compute_kernel, out_shape=(shape(2, 4, 4, 2, 8, 8, 128), s...  14.8 us
    pallas_call x2, local copies, waits for them, and re-layouts, per_device(): pl.pallas_call(functools.partial(sums_kernel, lats, lons), out_shape=(sha...  3.69 us

profile of v1, /device:TPU:1, one launch (start us, length us, event | category | flops | bytes accessed | tf_op | source)
XLA Modules:
  0.0 123.3 jit_solution(3728804823775143411)
XLA Ops:
  0.6 0.0 copy-start
  0.7 1.4 %copy.34.region = s32[2,12,6]{2,1,0:T(8,128)} copy(s32[2,12,6]{1,0,2:T(2,128)} %param.22) | data formatting | bytes 1152 | tf_op args[3]
  2.1 1.6 %copy.35.table = f32[1,6,6336]{2,1,0:T(8,128)} copy(f32[1,6,6336]{2,0,1:T(1,128)} %param.27) | data formatting | bytes 304128 | tf_op args[8]
  3.7 1.8 %copy.32.fields = f32[2,2,12,6,192]{4,3,2,1,0:T(8,128)} copy(f32[2,2,12,6,192]{4,1,3,2,0:T(2,128)} %param.19) | data formatting | bytes 442368 | tf_op args[0]
  5.5 1.8 %copy.33.cot = f32[2,2,12,6,192]{4,3,2,1,0:T(8,128)} copy(f32[2,2,12,6,192]{4,1,3,2,0:T(2,128)} %param.20) | data formatting | bytes 442368 | tf_op args[1]
  7.2 33.6 %halo_in.1 = (f32[144,384]{1,0:T(8,128)}, f32[144,384]{1,0:T(8,128)}) custom-call(s32[2,2]{1,0:T(2,128)} %keep.5, f32[2,2,12,6,192]{4,3,2,1,0:T(8,128)} %copy.32.fields, f32[2,2,12,6,192]{4,3,2,1,0:T(8,128)} %copy.33.cot), custom_call_target="tpu_custom_call" | custom-call | tf_op jit(solution)/shard_map/halo_in/pallas_call | solution.py:533
  40.9 0.0 copy-done
  40.9 1.2 copy.36.wout
  42.1 14.8 %block_both_ways.1 = (f32[2,4,4,2,8,8,128]{6,5,4,3,2,1,0:T(8,128)}, f32[16,24,128]{2,1,0:T(8,128)}, f32[4,36,192]{2,1,0:T(8,128)}, f32[144,192]{1,0:T(8,128)}) custom-call(s32[2,2]{1,0:T(2,128)} %keep.5, f32[144,384]{1,0:T(8,128)} %get-tuple-element.19.win, f32[144,384]{1,0:T(8,128)} %get-tuple-element.20.loc, s32[2,12,6]{2,1,0:T(8,128)} %copy.34.region, ...), custom_call_target="tpu_custom_call" | custom-call | tf_op jit(solution)/shard_map/block_both_ways/pallas_call | solution.py:547
  56.9 48.9 %gradient_sums.1 = (f32[2,2,12,6,192]{4,3,2,1,0:T(8,128)}, f32[192]{0:T(256)}, f32[192]{0:T(256)}, f32[6,576]{1,0:T(8,128)}, f32[576]{0:T(1024)}, /*index=5*/f32...) custom-call(s32[2,2]{1,0:T(2,128)} %keep.5, ...), custom_call_target="tpu_custom_call" | custom-call | tf_op jit(solution)/shard_map/gradient_sums/pallas_call | solution.py:567
  105.8 1.9 %copy.37 = f32[2,2,12,6,192]{4,1,3,2,0:T(2,128)} copy(f32[2,2,12,6,192]{4,3,2,1,0:T(8,128)} %get-tuple-element.25) | data formatting | bytes 442368 | tf_op jit(solution)/shard_map/gradient_sums/pallas_call | solution.py:567
  107.7 1.8 %copy.38 = f32[1,6,6336]{2,0,1:T(1,128)} copy(f32[1,6,6336]{2,1,0:T(8,128)} %get-tuple-element.30) | data formatting | bytes 304128 | tf_op jit(solution)/shard_map/gradient_sums/pallas_call | solution.py:567
  109.5 1.2 copy.50
  110.7 1.2 copy.51
  111.9 1.3 %copy.52 = f32[6,576]{1,0:T(8,128)} copy(f32[6,576]{1,0:T(8,128)} %get-tuple-element.54) | data formatting | bytes 27648
  113.3 1.3 %copy.53 = f32[576]{0:T(1024)} copy(f32[576]{0:T(1024)} %get-tuple-element.55) | data formatting | bytes 4608
  114.5 1.3 %copy.54 = f32[6,192]{1,0:T(8,128)} copy(f32[6,192]{1,0:T(8,128)} %get-tuple-element.57) | data formatting | bytes 9216
  115.8 1.2 copy.55
  117.0 1.2 copy.56
  118.2 1.2 copy.57
  119.4 1.3 %copy.58 = f32[6,768]{1,0:T(8,128)} copy(f32[6,768]{1,0:T(8,128)} %get-tuple-element.61) | data formatting | bytes 36864
  120.7 1.3 %copy.59 = f32[768]{0:T(1024)} copy(f32[768]{0:T(1024)} %get-tuple-element.62) | data formatting | bytes 6144
  122.0 1.3 %copy.60 = f32[24,192]{1,0:T(8,128)} copy(f32[24,192]{1,0:T(8,128)} %get-tuple-element.63) | data formatting | bytes 36864
Async XLA Ops:
  0.6 40.2 %copy-start = (f32[768,192]{0,1:T(8,128)S(1)}, f32[768,192]{0,1:T(8,128)}, u32[]{:S(2)}) copy-start(f32[768,192]{0,1:T(8,128)} %param.34) | copy-start | bytes 1769476

commit v2 on v1

v2 whole, which is shorter than its diff:
```python
import functools
import math

import jax
import jax.numpy as jnp
import numpy as np
from jax import lax
from jax.experimental import pallas as pl
from jax.experimental.pallas import tpu as pltpu
from jax.sharding import PartitionSpec as P

f32 = jnp.float32
bf16 = jnp.bfloat16
MESH = pl.DeviceIdType.MESH
C = 192
HEADS = 6
HID = 768
TOK = 144
ZH = 24
REL = 11
FLAT = 132
eps = 1e-05
kept = 1.25
scale = 1.0 / math.sqrt(32.0)
VMEM_LIMIT = 56 * 1024 * 1024


def bias_order():
    to = np.zeros((384, 384), np.float32)
    rest = np.zeros((384, 128), np.float32)
    for z in range(2):
        for h in range(12):
            for r in range(REL):
                lane = z * FLAT + h * REL + r
                spot = (REL - 1 - r) * ZH + h * 2 + 1 - z
                to[lane, spot] = 1.0
                if lane >= 256:
                    for head in range(HEADS):
                        rest[spot, 8 * head + lane - 256] = 1.0
    return to, rest


def spread_order():
    to = np.zeros((C, 256), np.float32)
    for feature in range(C):
        to[feature, 8 * (feature // 6) + feature % 6] = 1.0
    return to


def halves(values):
    high = values.astype(bf16)
    return high, (values - high.astype(f32)).astype(bf16)


def thirds(values):
    high = values.astype(bf16)
    left = values - high.astype(f32)
    mid = left.astype(bf16)
    return high, mid, (left - mid.astype(f32)).astype(bf16)


def one(a, b, ca, cb):
    return lax.dot_general(a, b, (((ca,), (cb,)), ((), ())), preferred_element_type=f32)


def product(a, b, ca=1, cb=0):
    return one(a[0], b[0], ca, cb) + (one(a[0], b[1], ca, cb) + one(a[1], b[0], ca, cb))


def norm_parts(values):
    center = values - jnp.mean(values, axis=-1, keepdims=True)
    spread = jnp.mean(center * center, axis=-1, keepdims=True)
    inv = lax.rsqrt(spread + eps)
    return center * inv, inv


def norm_back(grad, gain, unit, inv):
    scaled = grad * gain
    return inv * (
        scaled
        - jnp.mean(scaled, axis=-1, keepdims=True)
        - unit * jnp.mean(scaled * unit, axis=-1, keepdims=True)
    )


def neighbour(lat, lon, lats, lons, dlat, dlon):
    return lax.rem(lat + dlat + lats, lats), lax.rem(lon + dlon + lons, lons)


def take_tokens(read):
    return jnp.concatenate([read(w).reshape(ZH, C) for w in range(6)], axis=0)


def put_tokens(write, values):
    for w in range(6):
        write(w, values[w * ZH : (w + 1) * ZH, :].reshape(12, 2, C))


def kernel_a(
    lats, lons,
    keep, fields, cotg, region, n1g, n1s, wqkv, bqkv, table, wproj, bproj, n2g, n2s, win_w, b_in, wout,
    order, rest, spread,
    gather, table_o, back, other,
    sel_x, sel_c, win_x, win_c, dxa,
    early, late, pair_e, pair_l, a_e, a_l, b_e, b_l, acc_ae, acc_al, acc_b, z_in, mine,
    tabs, tab_rx, tab_pair, tab_sum, tab_all, wide_s,
    tab_in, bias_s, attn_s, diff_s, qp_s, mi_s, mo_s, row_s, tab_s,
    hx_ss, hx_rs, hc_ss, hc_rs, back_ss, back_rs, pe_ss, pe_rs, pl_ss, pl_rs, ae_ss, ae_rs, al_ss, al_rs,
    be_ss, be_rs, bl_ss, bl_rs, z_ss, z_rs, g_ss, g_rs, t_ss, t_rs, tp_ss, tp_rs, tg_ss, tg_rs,
):
    lat = lax.axis_index("lat")
    lon = lax.axis_index("lon")
    core = lax.rem(lat, 2)
    zl = lat // 2
    zh = lon // 16
    plane = lax.rem(lon, 16)
    px = plane // 4
    py = lax.rem(plane, 4)
    at = functools.partial(neighbour, lat, lon, lats, lons)
    every = []

    def send(src, dst, ss, rs, device):
        copy = pltpu.make_async_remote_copy(
            src_ref=src, dst_ref=dst, send_sem=ss, recv_sem=rs, device_id=device, device_id_type=MESH
        )
        copy.start()
        every.append(copy)
        return copy

    barrier = pltpu.get_barrier_semaphore()

    def hello(device):
        pl.semaphore_signal(barrier, inc=1, device_id=device, device_id_type=MESH)

    hello(at(1, 1))
    hello(at(0, 1))
    hello(at(-1, -1))
    hello(at(0, -1))
    hello(at(1, 0))
    hello(at(-1, 0))
    for d in range(8):
        hello((lax.rem(lat + 2 * d, 16), lax.rem(lon + 16, 32)))
    for d in range(1, 16):
        hello((lax.rem(lat + d, 16), lon))
        hello((lat, zh * 16 + lax.rem(plane + d, 16)))

    attn_sample = 1 - keep[0, 0]
    sel_x[...] = fields[attn_sample]
    sel_c[...] = cotg[attn_sample]
    win_x[0:6, 0:3] = sel_x[6:12, 3:6]
    win_c[0:6, 0:3] = sel_c[6:12, 3:6]

    tab_in[...] = jnp.zeros(tab_in.shape, f32)
    for zn in range(2):
        for hn in range(12):
            spot = hn * 2 + 1 - zn
            for zm in range(2):
                start = ((zn * 2 + zm) * 12 + hn) * FLAT
                tab_in[spot * 8 : spot * 8 + HEADS, zm * FLAT : (zm + 1) * FLAT] = jnp.concatenate(
                    [table[h, :, start : start + FLAT] for h in range(HEADS)], axis=0
                )
    shifted = None
    for part in thirds(tab_in[...]):
        term = one(part, order[...], 1, 0)
        shifted = term if shifted is None else shifted + term
    for l in range(3):
        bias_s[l] = shifted[:, l * 128 : l * 128 + 128]

    marks = jnp.concatenate([region[w] for w in range(6)], axis=0).astype(bf16)
    pick = lax.broadcasted_iota(jnp.int32, (ZH, 12), 0) // 2 == lax.broadcasted_iota(jnp.int32, (ZH, 12), 1)
    marks = one(pick.astype(bf16), marks, 1, 1)
    lane12 = lax.broadcasted_iota(jnp.int32, (ZH, 12), 1)
    level = 1 - (lax.broadcasted_iota(jnp.int32, (ZH, 12), 0) & 1)
    columns = []
    for w in range(6):
        column = jnp.sum(jnp.where(lane12 == 2 * w + level, marks, 0.0), axis=1, keepdims=True)
        columns.append(jnp.broadcast_to(column, (ZH, TOK)))
    mark_rows = jnp.concatenate(columns, axis=0)
    same = mark_rows == mark_rows.T

    w_qkv = halves(wqkv[...])
    w_proj = halves(wproj[...])
    w_in = halves(win_w[...])
    w_out = halves(wout[...])

    pl.semaphore_wait(barrier, 6 + 30 + 8)
    halo_x = []
    halo_c = []
    for copies, src, dst, ss, rs in ((halo_x, sel_x, win_x, hx_ss, hx_rs), (halo_c, sel_c, win_c, hc_ss, hc_rs)):
        for slot, (sh, sw) in enumerate(((0, 0), (1, 0), (0, 1))):
            copies.append(
                send(
                    src.at[pl.ds(sh * 6, 6), pl.ds(sw * 3, 3)],
                    dst.at[pl.ds(6 - sh * 6, 6), pl.ds(3 - sw * 3, 3)],
                    ss.at[slot], rs.at[slot],
                    at(sh - 1, sw - 1),
                )
            )
    for copy in halo_x:
        copy.wait_recv()

    x = take_tokens(lambda w: win_x[:, w])
    unit1, inv1 = norm_parts(x)
    gain1 = n1g[...].reshape(1, C)
    normed1 = halves(unit1 * gain1 + n1s[...].reshape(1, C))
    proj = product(normed1, w_qkv) + bqkv[...].reshape(1, 3 * C)
    query = halves(proj[:, 0:C] * scale)
    key = halves(proj[:, C : 2 * C])
    value = halves(proj[:, 2 * C : 3 * C])
    lanes = lax.broadcasted_iota(jnp.int32, (1, C), 1)
    masks = [(lanes // 32 == h) for h in range(HEADS)]

    def masked(pair, h):
        zero = jnp.zeros((), bf16)
        return tuple(jnp.where(masks[h], part, zero) for part in pair)

    mixed = jnp.zeros((TOK, C), f32)
    for h in range(HEADS):
        scores = product(masked(query, h), key, 1, 1)
        strip = jnp.concatenate([bias_s[l, pl.ds(h, ZH, stride=8), :] for l in range(3)], axis=1)
        bias = jnp.concatenate(
            [pltpu.roll(strip, (384 - (5 - wn) * ZH) % 384, axis=1)[:, 0:TOK] for wn in range(6)], axis=0
        )
        scores = jnp.where(same, scores + bias, -1e30)
        scores = jnp.exp(scores - jnp.max(scores, axis=-1, keepdims=True))
        attn = scores / jnp.sum(scores, axis=-1, keepdims=True)
        attn_s[h] = attn
        mixed = mixed + product(halves(attn), masked(value, h))
    mixed = halves(mixed)
    branch = product(mixed, w_proj) + bproj[...].reshape(1, C)

    for copy in halo_c:
        copy.wait_recv()
    cot = take_tokens(lambda w: win_c[:, w])
    both = keep[0, 0] == keep[0, 1]
    loc_x = take_tokens(lambda w: fields[1 - attn_sample, :, w])
    loc_cot = take_tokens(lambda w: cotg[1 - attn_sample, :, w])
    middle = jnp.where(both, x + kept * branch, loc_x)
    cot_m = jnp.where(both, cot, loc_cot)
    unit2, inv2 = norm_parts(middle)
    gain2 = n2g[...].reshape(1, C)
    normed2 = halves(unit2 * gain2 + n2s[...].reshape(1, C))
    hidden = product(normed2, w_in) + b_in[...].reshape(1, HID)
    cdf = 0.5 * (1.0 + lax.erf(hidden * math.sqrt(0.5)))
    slope = cdf + hidden * jnp.exp(-0.5 * hidden * hidden) * (1.0 / math.sqrt(2.0 * math.pi))
    grad_y = halves(kept * cot_m)
    grad_hidden = halves(product(grad_y, w_out) * slope)
    mo_s[:, 0:C] = product(halves(hidden * cdf), grad_y, 0, 0)

    ones_lane = (lax.broadcasted_iota(jnp.int32, (1, 256), 1) & 7) == 6

    def spread_out(pair):
        high = one(pair[0], spread[...], 1, 0)
        low = one(pair[1], spread[...], 1, 0)
        return jnp.where(ones_lane, 1.0, high).astype(bf16), low.astype(bf16)

    mi_s[...] = product(spread_out(normed2), grad_hidden, 0, 0)

    low_lanes = lax.broadcasted_iota(jnp.int32, (8, 128), 1) < 64

    def put(buffer, count, j, tile_id, tile, rows=slice(None)):
        a = lax.rem(j // 4, 4)
        b = lax.rem(j, 4)
        if tile_id < count:
            buffer[0, a, b, j // 16, tile_id, rows, :] = tile
        else:
            buffer[1, b, a, j // 16, tile_id - count, rows, :] = tile

    def pack_early(j, carry):
        at8 = pl.ds(pl.multiple_of(j * 8, 8), 8)
        for t in range(6):
            put(early, 5, j, t, mi_s[at8, t * 128 : t * 128 + 128])
        tails = []
        for k in range(3):
            rows = pl.ds(pl.multiple_of(j * 24 + k * 8, 8), 8)
            put(early, 5, j, 6 + k, mo_s[rows, 0:128])
            tails.append(mo_s[rows, 128:256])
        put(early, 5, j, 9, jnp.where(low_lanes, tails[0], pltpu.roll(tails[1], 64, axis=1)))
        pairs = jnp.where(low_lanes, tails[2], pltpu.roll(pltpu.roll(tails[2], 64, axis=1), 7, axis=0))
        for k in range(4):
            put(early, 5, j, k, pairs[2 * k : 2 * k + 1, :], slice(7, 8))
        return carry

    lax.fori_loop(0, 32, pack_early, 0)
    twin = (lat + 1 - 2 * core, lon)
    pair_early = send(early.at[1 - core], pair_e, pe_ss, pe_rs, twin)

    grad_n2 = product(grad_hidden, w_in, 1, 1)
    row_s[0:1, 2 * C : 3 * C] = jnp.sum(grad_n2 * unit2, axis=0, keepdims=True)
    row_s[0:1, 3 * C : 4 * C] = jnp.sum(grad_n2, axis=0, keepdims=True)
    grad_m = cot_m + norm_back(grad_n2, gain2, unit2, inv2)
    grad_a = jnp.where(both, grad_m, cot)

    def put_other(w, block):
        other[:, w] = block

    put_tokens(put_other, jnp.where(both, loc_cot, grad_m))

    first = px + core * (py - px)
    second = py + core * (px - py)

    def along(pos_first, pos_second):
        x_pos = pos_first + core * (pos_second - pos_first)
        y_pos = pos_second + core * (pos_first - pos_second)
        return lat, zh * 16 + x_pos * 4 + y_pos

    def add_pair(buffer, arrived):
        def step(i, carry):
            for j in range(4):
                arrived[i, j] = arrived[i, j] + buffer[core, i, j]
            return carry

        lax.fori_loop(0, 4, step, 0)

    def send_first(arrived, slots, ss, rs):
        copies = []
        for d in range(1, 4):
            to = lax.rem(first + d, 4)
            copies.append(send(arrived.at[to], slots.at[d - 1], ss.at[d - 1], rs.at[d - 1], along(to, second)))
        return copies

    def add_first(arrived, slots, acc):
        for j in range(4):
            acc[j] = (arrived[first, j] + slots[0, j]) + (slots[1, j] + slots[2, j])

    def send_second(acc, slots, ss, rs):
        copies = []
        for d in range(1, 4):
            to = lax.rem(second + d, 4)
            copies.append(send(acc.at[to], slots.at[d - 1], ss.at[d - 1], rs.at[d - 1], along(first, to)))
        return copies

    grad_b = halves(kept * grad_a)
    qp_s[:, 3 * C : 4 * C] = product(spread_out(mixed), grad_b, 0, 0)
    grad_o = halves(product(grad_b, w_proj, 1, 1))
    grad_q = jnp.zeros((TOK, C), f32)
    grad_k = jnp.zeros((TOK, C), f32)
    grad_v = jnp.zeros((TOK, C), f32)
    diff_s[...] = jnp.zeros(diff_s.shape, f32)
    first_early = None
    for h in range(HEADS):
        attn = attn_s[h]
        grad_oh = masked(grad_o, h)
        grad_attn = product(grad_oh, value, 1, 1)
        grad_v = grad_v + product(halves(attn), grad_oh, 0, 0)
        term = attn * grad_attn
        grad_s = term - attn * jnp.sum(term, axis=-1, keepdims=True)
        grad_sp = halves(grad_s)
        grad_q = grad_q + product(grad_sp, masked(key, h))
        grad_k = grad_k + product(grad_sp, masked(query, h), 0, 0)
        wide = jnp.concatenate([grad_s, jnp.zeros((TOK, 384 - TOK), f32)], axis=1)
        total = None
        for wn in range(6):
            block = wide[wn * ZH : (wn + 1) * ZH, :]
            if wn < 5:
                block = pltpu.roll(block, (5 - wn) * ZH, axis=1)
            total = block if total is None else total + block
        for l in range(3):
            diff_s[l, pl.ds(h, ZH, stride=8), :] = total[:, l * 128 : l * 128 + 128]
        if h == 1:
            pair_early.wait_recv()
            add_pair(early, pair_e)
            first_early = send_first(pair_e, a_e, ae_ss, ae_rs)
    grad_p = halves(jnp.concatenate([grad_q * scale, grad_k, grad_v], axis=1))
    qp_s[:, 0 : 3 * C] = product(spread_out(normed1), grad_p, 0, 0)
    grad_n1 = product(grad_p, w_qkv, 1, 1)
    row_s[0:1, 0:C] = jnp.sum(grad_n1 * unit1, axis=0, keepdims=True)
    row_s[0:1, C : 2 * C] = jnp.sum(grad_n1, axis=0, keepdims=True)

    def pack_late(j, carry):
        at8 = pl.ds(pl.multiple_of(j * 8, 8), 8)
        last = lax.broadcasted_iota(jnp.int32, (8, 128), 0) == 7
        for t in range(6):
            part = slice(t * 128, t * 128 + 128)
            put(late, 3, j, t, jnp.where(last, row_s[0:1, part], qp_s[at8, part]))
        return carry

    lax.fori_loop(0, 32, pack_late, 0)
    pair_late = send(late.at[1 - core], pair_l, pl_ss, pl_rs, twin)

    grad_x = grad_a + norm_back(grad_n1, gain1, unit1, inv1)

    def put_dxa(w, block):
        dxa[:, w] = block

    put_tokens(put_dxa, grad_x)
    home = []
    for slot, (hh, wh) in enumerate(((1, 1), (0, 1), (1, 0))):
        home.append(
            send(
                dxa.at[pl.ds(hh * 6, 6), pl.ds(wh * 3, 3)],
                back.at[pl.ds(6 - hh * 6, 6), pl.ds(3 - wh * 3, 3)],
                back_ss.at[slot], back_rs.at[slot], at(hh, wh),
            )
        )
    back[6:12, 3:6] = dxa[0:6, 0:3]

    diff = halves(jnp.concatenate([diff_s[l] for l in range(3)], axis=1))
    lanes_back = one(diff[0], order[...], 1, 1) + one(diff[1], order[...], 1, 1)
    tail = one(diff[0], rest[...], 1, 0) + one(diff[1], rest[...], 1, 0)
    row_id = lax.broadcasted_iota(jnp.int32, tail.shape, 0) & 7
    lane_id = lax.broadcasted_iota(jnp.int32, tail.shape, 1) // 8
    tail = jnp.where(row_id == lane_id, tail, 0.0).reshape(ZH, 8, 128).sum(axis=1)
    for l in range(2):
        tab_s[l] = lanes_back[:, l * 128 : l * 128 + 128]
    tab_s[0, pl.ds(6, ZH, stride=8), :] = tail
    for k in range(8):
        for l in range(2):
            tabs[2 * k + l] = tab_s[l, 24 * k : 24 * k + 24, :]

    pair_late.wait_recv()
    add_pair(late, pair_l)
    first_late = send_first(pair_l, a_l, al_ss, al_rs)
    tab_copies = []
    for d in range(1, 16):
        to = lax.rem(plane + d, 16)
        tab_copies.append(send(tabs.at[to], tab_rx.at[d - 1], t_ss.at[d - 1], t_rs.at[d - 1], (lat, zh * 16 + to)))

    for copy in first_early:
        copy.wait_recv()
    add_first(pair_e, a_e, acc_ae)
    second_early = send_second(acc_ae, b_e, be_ss, be_rs)

    for copy in first_late:
        copy.wait_recv()
    add_first(pair_l, a_l, acc_al)
    second_late = send_second(acc_al, b_l, bl_ss, bl_rs)

    for copy in tab_copies:
        copy.wait_recv()
    total = tabs[plane]
    for d in range(15):
        total = total + tab_rx[d]
    tab_sum[...] = total
    tab_across = send(tab_sum, tab_pair, tp_ss, tp_rs, (lat, lax.rem(lon + 16, 32)))

    for copy in second_early:
        copy.wait_recv()
    acc_b[:, 3:8] = (acc_ae[second] + b_e[0]) + (b_e[1] + b_e[2])
    for copy in second_late:
        copy.wait_recv()
    acc_b[:, 0:3] = (acc_al[second] + b_l[0]) + (b_l[1] + b_l[2])
    z_copies = []
    for d in (8, 7, 9, 6, 10, 5, 11, 4, 12, 3, 13, 2, 14, 1, 15):
        to = lax.rem(zh * 8 + zl + d, 16)
        z_copies.append(
            send(
                acc_b.at[to // 8, lax.rem(to, 8)], z_in.at[d - 1], z_ss.at[d - 1], z_rs.at[d - 1],
                (lax.rem(to, 8) * 2 + core, (to // 8) * 16 + plane),
            )
        )

    tab_across.wait_recv()
    tab_all[plane] = tab_sum[...] + tab_pair[...]
    tab_back = []
    for d in range(1, 16):
        to = lax.rem(plane + d, 16)
        tab_back.append(
            send(tab_all.at[plane], tab_all.at[plane], tg_ss.at[d - 1], tg_rs.at[d - 1], (lat, zh * 16 + to))
        )

    for copy in z_copies:
        copy.wait_recv()
    total = acc_b[zh, zl]
    for d in range(15):
        total = total + z_in[d]
    slot = core * 8 + zl
    mine[...] = total
    gather[slot] = total
    g_copies = []
    for d in range(1, 16):
        to = lax.rem(lat + d, 16)
        g_copies.append(send(mine, gather.at[slot], g_ss.at[d - 1], g_rs.at[d - 1], (to, lon)))

    for copy in tab_back:
        copy.wait_recv()
    for k in range(8):
        for l in range(2):
            wide_s[l, 24 * k : 24 * k + 24, :] = tab_all[2 * k + l]
    tail = wide_s[0, pl.ds(6, ZH, stride=8), :]
    for h in range(HEADS):
        moved = tail if h == 0 else pltpu.roll(tail, 128 - 8 * h, axis=1)
        wide_s[2, pl.ds(h, ZH, stride=8), :] = moved
    for zn in range(2):
        for hn in range(12):
            spot = hn * 2 + 1 - zn
            block = jnp.concatenate([wide_s[l, spot * 8 : spot * 8 + 8, :] for l in range(3)], axis=1)
            for zm in range(2):
                start = ((zn * 2 + zm) * 12 + hn) * FLAT
                for h in range(HEADS):
                    table_o[h, :, start : start + FLAT] = block[h : h + 1, zm * FLAT : (zm + 1) * FLAT]

    for copy in home:
        copy.wait_recv()
    for copy in g_copies:
        copy.wait_recv()
    for copy in every:
        copy.wait_send()


def kernel_b(
    keep, gather, table_i, back, other,
    fields_grad, n1g_o, n1s_o, qkvw_o, qkvb_o, table_o, projw_o, projb_o, n2g_o, n2s_o, inw_o, inb_o, outw_o,
):
    table_o[...] = table_i[...]
    first_kept = keep[0, 0] == 1
    fields_grad[0] = jnp.where(first_kept, back[...], other[...])
    fields_grad[1] = jnp.where(first_kept, other[...], back[...])

    def late(t):
        return gather.at[(t // 3) * 8 + t % 3]

    def early(t):
        return gather.at[(t // 5) * 8 + 3 + t % 5]

    def strip(tile, row, rows):
        return jnp.concatenate([tile(t)[row : row + rows, :] for t in range(6)], axis=1)

    sums = strip(late, 0, 6)
    qkvw_o[...] = sums[:, 0 : 3 * C]
    projw_o[...] = sums[:, 3 * C : 4 * C]
    inw_o[...] = strip(early, 0, 6)
    small = strip(late, 6, 1)
    qkvb_o[...] = small[:, 0 : 3 * C].reshape(3 * C)
    projb_o[...] = small[:, 3 * C : 4 * C].reshape(C)
    inb_o[...] = strip(early, 6, 1).reshape(HID)
    norms = strip(late, 7, 1)
    for i, ref in enumerate((n1g_o, n1s_o, n2g_o, n2s_o)):
        ref[...] = norms[:, i * C : (i + 1) * C].reshape(C)
    for k in range(3):
        outw_o[8 * k : 8 * k + 8, 0:128] = early(6 + k)[...]
    mix = early(9)[...]
    outw_o[0:8, 128:192] = mix[:, 0:64]
    outw_o[8:16, 128:192] = pltpu.roll(mix, 64, axis=1)[:, 0:64]
    for k in range(4):
        line = early(k)[7:8, :]
        outw_o[16 + 2 * k : 17 + 2 * k, 128:192] = line[:, 0:64]
        outw_o[17 + 2 * k : 18 + 2 * k, 128:192] = pltpu.roll(line, 64, axis=1)[:, 0:64]


def shape(*dims):
    return jax.ShapeDtypeStruct(dims, f32)


def vmem():
    return pl.BlockSpec(memory_space=pltpu.VMEM)


def smem():
    return pl.BlockSpec(memory_space=pltpu.SMEM)


def per_device(lats, lons, fields, cotangent, keep_mask, region_ids, *weights):
    order, rest = (jnp.asarray(m, bf16) for m in bias_order())
    spread = jnp.asarray(spread_order(), bf16)
    weights = list(weights)
    weights[4] = weights[4].transpose(1, 0, 2)
    weights[-1] = weights[-1].T
    grid_order = (0, 2, 3, 1, 4)
    one_sem = pltpu.SemaphoreType.DMA

    def sems(count):
        return pltpu.SemaphoreType.DMA((count,))

    def buf(*dims):
        return pltpu.VMEM(dims, f32)

    tile = (8, 128)
    block = (12, 6, 2, C)
    packed = pl.pallas_call(
        functools.partial(kernel_a, lats, lons),
        out_shape=(shape(16, 8, 128), shape(*(HEADS, 1, 6336)), shape(*block), shape(*block)),
        in_specs=[smem()] + [vmem()] * 18,
        out_specs=(vmem(),) * 4,
        scratch_shapes=[
            buf(*block), buf(*block), buf(*block), buf(*block), buf(*block),
            buf(2, 4, 4, 2, 5, *tile), buf(2, 4, 4, 2, 3, *tile),
            buf(4, 4, 2, 5, *tile), buf(4, 4, 2, 3, *tile),
            buf(3, 4, 2, 5, *tile), buf(3, 4, 2, 3, *tile),
            buf(3, 2, 5, *tile), buf(3, 2, 3, *tile),
            buf(4, 2, 5, *tile), buf(4, 2, 3, *tile),
            buf(2, 8, *tile), buf(15, *tile), buf(*tile),
            buf(16, 24, 128), buf(15, 24, 128), buf(24, 128), buf(24, 128), buf(16, 24, 128), buf(3, 192, 128),
            buf(192, 384), buf(3, 192, 128), buf(HEADS, TOK, TOK), buf(3, 192, 128),
            buf(256, 768), buf(256, 768), buf(768, 256), buf(8, 768), buf(2, 192, 128),
            sems(3), sems(3), sems(3), sems(3), sems(3), sems(3),
            one_sem, one_sem, one_sem, one_sem,
            sems(3), sems(3), sems(3), sems(3), sems(3), sems(3), sems(3), sems(3),
            sems(15), sems(15), sems(15), sems(15), sems(15), sems(15), one_sem, one_sem, sems(15), sems(15),
        ],
        compiler_params=pltpu.CompilerParams(collective_id=0, has_side_effects=True, vmem_limit_bytes=VMEM_LIMIT),
        name="block_both_ways",
    )(
        keep_mask, fields.transpose(grid_order), cotangent.transpose(grid_order), region_ids.transpose(2, 0, 1),
        *weights, order, rest, spread,
    )
    outs = list(
        pl.pallas_call(
            kernel_b,
            out_shape=(
                shape(2, *block), shape(C), shape(C), shape(6, 3 * C), shape(3 * C), shape(*(HEADS, 1, 6336)),
                shape(6, C), shape(C), shape(C), shape(C), shape(6, HID), shape(HID), shape(24, C),
            ),
            in_specs=[smem()] + [vmem()] * 4,
            out_specs=(vmem(),) * 13,
            compiler_params=pltpu.CompilerParams(vmem_limit_bytes=VMEM_LIMIT),
            name="unpack",
        )(keep_mask, *packed)
    )
    outs[0] = outs[0].transpose(0, 3, 1, 2, 4)
    outs[5] = outs[5].transpose(1, 0, 2)
    return tuple(outs)


def solution(mesh):
    grid = P(None, None, "lat", "lon", None)
    rows = P("lon", None)
    return jax.shard_map(
        functools.partial(per_device, mesh.shape["lat"], mesh.shape["lon"]),
        mesh=mesh,
        in_specs=(grid, grid, P(), P(None, "lat", "lon"), P(), P(), P(), P(), P("lat", None, None))
        + (P(),) * 7,
        out_specs=(grid, P(), P(), rows, P(), P("lat", None, None), rows, P(), P(), P(), rows, P(), rows),
        check_vma=False,
    )
```

time: 124 us -> 83.2 us (0.67)
  local copies, waits for them, and re-layouts: 25.3 us -> 0 us
  Pallas kernels: 97.3 us -> 82.4 us
    unnamed x18 -> x0, local copies, waits for them, and re-layouts: 21.6 us -> none
    pallas_call x3 -> x2, Pallas kernels: 97.3 us -> 82.4 us  [the longest x1 80.4 us: per_device(): pl.pallas_call(functools.partial(kernel_a, lats, lons), out_shape=(shape(...]
    pallas_call x2 -> x0, local copies, waits for them, and re-layouts: 3.69 us -> none  [per_device(): pl.pallas_call(functools.partial(sums_kernel, lats, lons), out_shape=(sha...]
where the time goes in v2:
time: 83.2 us; the launch traced here: 83 us
  Pallas kernels  82.4 us (99%)
    pallas_call x1, Pallas kernels, per_device(): pl.pallas_call(functools.partial(kernel_a, lats, lons), out_shape=(shape(...  80.4 us
    pallas_call x1, Pallas kernels, per_device(): pl.pallas_call(kernel_b, out_shape=(shape(2, *block), shape(C), shape(C),...  1.93 us

profile of v2, /device:TPU:1, one launch (start us, length us, event | category | flops | bytes accessed | tf_op | source)
XLA Modules:
  0.0 83.0 jit_solution(13795581995864360060)
XLA Ops:
  0.7 80.4 %block_both_ways.1 = (f32[16,8,128]{2,1,0:T(8,128)}, f32[6,1,6336]{2,1,0:T(1,128)}, f32[12,6,2,192]{3,2,1,0:T(2,128)}, f32[12,6,2,192]{3,2,1,0:T(2,128)}) custom-call(s32[2,2]{1,0:T(2,128)} %keep.3, f32[2,12,6,2,192]{4,3,2,1,0:T(2,128)} %bitcast.8, f32[2,12,6,2,192]{4,3,2,1,0:T(2,128)} %bitcast.9, s32[6,2,12]{2,1,0:T(2,128)} %bitcast.11, f32[192]{0:T(256)} %n1g.1, ...), custom_call_target="tpu_custom_call" | custom-call | tf_op jit(solution)/shard_map/block_both_ways/pallas_call | solution.py:570
  81.1 1.9 %unpack.1 = (f32[2,12,6,2,192]{4,3,2,1,0:T(2,128)}, f32[192]{0:T(256)}, f32[192]{0:T(256)}, f32[6,576]{1,0:T(8,128)}, f32[576]{0:T(1024)}, /*index=5*/f32[6,1,63...) custom-call(s32[2,2]{1,0:T(2,128)} %keep.3, ...), custom_call_target="tpu_custom_call" | custom-call | tf_op jit(solution)/shard_map/unpack/pallas_call | solution.py:598

commit v3 on v2

--- a/solution.py
+++ b/solution.py
@@ -98,14 +98,24 @@
 
 def kernel_a(
     lats, lons,
-    keep, fields, cotg, region, n1g, n1s, wqkv, bqkv, table, wproj, bproj, n2g, n2s, win_w, b_in, wout,
+    keep, *refs,
+):
+    hbm, refs = refs[0:18], refs[18:]
+    results, refs = refs[0:4], refs[4:]
+    loaded, refs = refs[0:18], refs[18:]
+    compute_and_sum(lats, lons, keep, hbm, loaded, *results, *loaded, *refs)
+
+
+def compute_and_sum(
+    lats, lons, keep, hbm, loaded,
+    gather, table_o, back, other,
+    fields, cotg, region, n1g, n1s, wqkv, bqkv, table, wproj, bproj, n2g, n2s, win_w, b_in, wout,
     order, rest, spread,
-    gather, table_o, back, other,
-    sel_x, sel_c, win_x, win_c, dxa,
+    load_sem, sel_x, sel_c, win_x, win_c, dxa, region_win,
     early, late, pair_e, pair_l, a_e, a_l, b_e, b_l, acc_ae, acc_al, acc_b, z_in, mine,
     tabs, tab_rx, tab_pair, tab_sum, tab_all, wide_s,
-    tab_in, bias_s, attn_s, diff_s, qp_s, mi_s, mo_s, row_s, tab_s,
-    hx_ss, hx_rs, hc_ss, hc_rs, back_ss, back_rs, pe_ss, pe_rs, pl_ss, pl_rs, ae_ss, ae_rs, al_ss, al_rs,
+    tab_in, bias_s, attn_s, diff_s, qp_s, row_s, tab_s,
+    hx_ss, hx_rs, hc_ss, hc_rs, reg_ss, reg_rs, back_ss, back_rs, pe_ss, pe_rs, pl_ss, pl_rs, ae_ss, ae_rs, al_ss, al_rs,
     be_ss, be_rs, bl_ss, bl_rs, z_ss, z_rs, g_ss, g_rs, t_ss, t_rs, tp_ss, tp_rs, tg_ss, tg_rs,
 ):
     lat = lax.axis_index("lat")
@@ -132,23 +142,50 @@
     def hello(device):
         pl.semaphore_signal(barrier, inc=1, device_id=device, device_id_type=MESH)
 
-    hello(at(1, 1))
+    hello(at(1, -1))
+    hello(at(0, -1))
+    hello(at(-1, 1))
     hello(at(0, 1))
-    hello(at(-1, -1))
-    hello(at(0, -1))
     hello(at(1, 0))
     hello(at(-1, 0))
-    for d in range(8):
-        hello((lax.rem(lat + 2 * d, 16), lax.rem(lon + 16, 32)))
+    for d in range(0, 16, 2):
+        hello((lax.rem(lat + d, 16), lax.rem(lon + 16, 32)))
     for d in range(1, 16):
         hello((lax.rem(lat + d, 16), lon))
         hello((lat, zh * 16 + lax.rem(plane + d, 16)))
 
+    loads = [pltpu.make_async_copy(hbm[i], loaded[i], load_sem.at[i]) for i in range(18)]
+    for i in (0, 1, 7, 15, 2, 5, 8, 12, 14, 16, 17, 3, 4, 6, 9, 10, 11, 13):
+        loads[i].start()
     attn_sample = 1 - keep[0, 0]
+    loads[0].wait()
+    loads[1].wait()
     sel_x[...] = fields[attn_sample]
     sel_c[...] = cotg[attn_sample]
-    win_x[0:6, 0:3] = sel_x[6:12, 3:6]
-    win_c[0:6, 0:3] = sel_c[6:12, 3:6]
+    win_x[0:6, 3:6] = sel_x[6:12, 0:3]
+    win_c[0:6, 3:6] = sel_c[6:12, 0:3]
+
+    halo_x = []
+    halo_c = []
+    quadrants = ((0, 1), (1, 1), (0, 0))
+
+    def start_halo(src, dst, ss, rs, copies):
+        for slot, (sh, sw) in enumerate(quadrants):
+            copies.append(
+                send(
+                    src.at[pl.ds(sh * 6, 6), pl.ds(sw * 3, 3)],
+                    dst.at[pl.ds(6 - sh * 6, 6), pl.ds(3 - sw * 3, 3)],
+                    ss.at[slot], rs.at[slot], at(sh - 1, sw),
+                )
+            )
+
+    pl.semaphore_wait(barrier, 6 + 30 + 8)
+    start_halo(sel_x, win_x, hx_ss, hx_rs, halo_x)
+    loads[2].wait()
+    regions = send(region, region_win, reg_ss, reg_rs, at(0, 1))
+
+    for i in (7, 15):
+        loads[i].wait()
 
     tab_in[...] = jnp.zeros(tab_in.shape, f32)
     for zn in range(2):
@@ -166,7 +203,19 @@
     for l in range(3):
         bias_s[l] = shifted[:, l * 128 : l * 128 + 128]
 
-    marks = jnp.concatenate([region[w] for w in range(6)], axis=0).astype(bf16)
+    for i in (5, 8, 12, 14, 16, 17, 3, 4, 6, 9, 10, 11, 13):
+        loads[i].wait()
+    w_qkv = halves(wqkv[...])
+    w_proj = halves(wproj[...])
+    w_in = halves(win_w[...])
+    w_out = halves(wout[...])
+
+    loc_x = take_tokens(lambda w: fields[1 - attn_sample, :, w])
+    loc_cot = take_tokens(lambda w: cotg[1 - attn_sample, :, w])
+    start_halo(sel_c, win_c, hc_ss, hc_rs, halo_c)
+
+    regions.wait_recv()
+    marks = jnp.concatenate([region_win[w] for w in range(6)], axis=0).astype(bf16)
     pick = lax.broadcasted_iota(jnp.int32, (ZH, 12), 0) // 2 == lax.broadcasted_iota(jnp.int32, (ZH, 12), 1)
     marks = one(pick.astype(bf16), marks, 1, 1)
     lane12 = lax.broadcasted_iota(jnp.int32, (ZH, 12), 1)
@@ -178,24 +227,6 @@
     mark_rows = jnp.concatenate(columns, axis=0)
     same = mark_rows == mark_rows.T
 
-    w_qkv = halves(wqkv[...])
-    w_proj = halves(wproj[...])
-    w_in = halves(win_w[...])
-    w_out = halves(wout[...])
-
-    pl.semaphore_wait(barrier, 6 + 30 + 8)
-    halo_x = []
-    halo_c = []
-    for copies, src, dst, ss, rs in ((halo_x, sel_x, win_x, hx_ss, hx_rs), (halo_c, sel_c, win_c, hc_ss, hc_rs)):
-        for slot, (sh, sw) in enumerate(((0, 0), (1, 0), (0, 1))):
-            copies.append(
-                send(
-                    src.at[pl.ds(sh * 6, 6), pl.ds(sw * 3, 3)],
-                    dst.at[pl.ds(6 - sh * 6, 6), pl.ds(3 - sw * 3, 3)],
-                    ss.at[slot], rs.at[slot],
-                    at(sh - 1, sw - 1),
-                )
-            )
     for copy in halo_x:
         copy.wait_recv()
 
@@ -233,8 +264,6 @@
         copy.wait_recv()
     cot = take_tokens(lambda w: win_c[:, w])
     both = keep[0, 0] == keep[0, 1]
-    loc_x = take_tokens(lambda w: fields[1 - attn_sample, :, w])
-    loc_cot = take_tokens(lambda w: cotg[1 - attn_sample, :, w])
     middle = jnp.where(both, x + kept * branch, loc_x)
     cot_m = jnp.where(both, cot, loc_cot)
     unit2, inv2 = norm_parts(middle)
@@ -245,7 +274,7 @@
     slope = cdf + hidden * jnp.exp(-0.5 * hidden * hidden) * (1.0 / math.sqrt(2.0 * math.pi))
     grad_y = halves(kept * cot_m)
     grad_hidden = halves(product(grad_y, w_out) * slope)
-    mo_s[:, 0:C] = product(halves(hidden * cdf), grad_y, 0, 0)
+    grad_out_w = product(halves(hidden * cdf), grad_y, 0, 0)
 
     ones_lane = (lax.broadcasted_iota(jnp.int32, (1, 256), 1) & 7) == 6
 
@@ -254,34 +283,32 @@
         low = one(pair[1], spread[...], 1, 0)
         return jnp.where(ones_lane, 1.0, high).astype(bf16), low.astype(bf16)
 
-    mi_s[...] = product(spread_out(normed2), grad_hidden, 0, 0)
+    grad_in_w = product(spread_out(normed2), grad_hidden, 0, 0)
 
     low_lanes = lax.broadcasted_iota(jnp.int32, (8, 128), 1) < 64
 
     def put(buffer, count, j, tile_id, tile, rows=slice(None)):
-        a = lax.rem(j // 4, 4)
-        b = lax.rem(j, 4)
+        zh_j, a, b = j // 16, j // 4 % 4, j % 4
         if tile_id < count:
-            buffer[0, a, b, j // 16, tile_id, rows, :] = tile
+            buffer[0, a, b, zh_j, tile_id, rows, :] = tile
         else:
-            buffer[1, b, a, j // 16, tile_id - count, rows, :] = tile
-
-    def pack_early(j, carry):
-        at8 = pl.ds(pl.multiple_of(j * 8, 8), 8)
+            buffer[1, b, a, zh_j, tile_id - count, rows, :] = tile
+
+    last_row = lax.broadcasted_iota(jnp.int32, (8, 128), 0) == 7
+    for j in range(32):
+        block = grad_out_w[24 * j : 24 * j + 24, :]
+        tails = [
+            jnp.concatenate([block[8 * k : 8 * k + 8, 128:192], jnp.zeros((8, 64), f32)], axis=1) for k in range(3)
+        ]
+        for k in range(3):
+            put(early, 5, j, 6 + k, block[8 * k : 8 * k + 8, 0:128])
+        put(early, 5, j, 9, tails[0] + pltpu.roll(tails[1], 64, axis=1))
+        pairs = tails[2] + pltpu.roll(pltpu.roll(tails[2], 64, axis=1), 7, axis=0)
         for t in range(6):
-            put(early, 5, j, t, mi_s[at8, t * 128 : t * 128 + 128])
-        tails = []
-        for k in range(3):
-            rows = pl.ds(pl.multiple_of(j * 24 + k * 8, 8), 8)
-            put(early, 5, j, 6 + k, mo_s[rows, 0:128])
-            tails.append(mo_s[rows, 128:256])
-        put(early, 5, j, 9, jnp.where(low_lanes, tails[0], pltpu.roll(tails[1], 64, axis=1)))
-        pairs = jnp.where(low_lanes, tails[2], pltpu.roll(pltpu.roll(tails[2], 64, axis=1), 7, axis=0))
-        for k in range(4):
-            put(early, 5, j, k, pairs[2 * k : 2 * k + 1, :], slice(7, 8))
-        return carry
-
-    lax.fori_loop(0, 32, pack_early, 0)
+            tile = grad_in_w[8 * j : 8 * j + 8, t * 128 : t * 128 + 128]
+            if t < 4:
+                tile = jnp.where(last_row, pairs[2 * t : 2 * t + 1, :], tile)
+            put(early, 5, j, t, tile)
     twin = (lat + 1 - 2 * core, lon)
     pair_early = send(early.at[1 - core], pair_e, pe_ss, pe_rs, twin)
 
@@ -305,12 +332,9 @@
         return lat, zh * 16 + x_pos * 4 + y_pos
 
     def add_pair(buffer, arrived):
-        def step(i, carry):
+        for i in range(4):
             for j in range(4):
                 arrived[i, j] = arrived[i, j] + buffer[core, i, j]
-            return carry
-
-        lax.fori_loop(0, 4, step, 0)
 
     def send_first(arrived, slots, ss, rs):
         copies = []
@@ -367,15 +391,10 @@
     row_s[0:1, 0:C] = jnp.sum(grad_n1 * unit1, axis=0, keepdims=True)
     row_s[0:1, C : 2 * C] = jnp.sum(grad_n1, axis=0, keepdims=True)
 
-    def pack_late(j, carry):
-        at8 = pl.ds(pl.multiple_of(j * 8, 8), 8)
-        last = lax.broadcasted_iota(jnp.int32, (8, 128), 0) == 7
+    for j in range(32):
         for t in range(6):
             part = slice(t * 128, t * 128 + 128)
-            put(late, 3, j, t, jnp.where(last, row_s[0:1, part], qp_s[at8, part]))
-        return carry
-
-    lax.fori_loop(0, 32, pack_late, 0)
+            put(late, 3, j, t, jnp.where(last_row, row_s[0:1, part], qp_s[8 * j : 8 * j + 8, part]))
     pair_late = send(late.at[1 - core], pair_l, pl_ss, pl_rs, twin)
 
     grad_x = grad_a + norm_back(grad_n1, gain1, unit1, inv1)
@@ -385,15 +404,15 @@
 
     put_tokens(put_dxa, grad_x)
     home = []
-    for slot, (hh, wh) in enumerate(((1, 1), (0, 1), (1, 0))):
+    for slot, (hh, wh) in enumerate(((1, 0), (0, 0), (1, 1))):
         home.append(
             send(
                 dxa.at[pl.ds(hh * 6, 6), pl.ds(wh * 3, 3)],
                 back.at[pl.ds(6 - hh * 6, 6), pl.ds(3 - wh * 3, 3)],
-                back_ss.at[slot], back_rs.at[slot], at(hh, wh),
+                back_ss.at[slot], back_rs.at[slot], at(hh, wh - 1),
             )
         )
-    back[6:12, 3:6] = dxa[0:6, 0:3]
+    back[6:12, 0:3] = dxa[0:6, 3:6]
 
     diff = halves(jnp.concatenate([diff_s[l] for l in range(3)], axis=1))
     lanes_back = one(diff[0], order[...], 1, 1) + one(diff[1], order[...], 1, 1)
@@ -408,14 +427,14 @@
         for l in range(2):
             tabs[2 * k + l] = tab_s[l, 24 * k : 24 * k + 24, :]
 
-    pair_late.wait_recv()
-    add_pair(late, pair_l)
-    first_late = send_first(pair_l, a_l, al_ss, al_rs)
     tab_copies = []
     for d in range(1, 16):
         to = lax.rem(plane + d, 16)
         tab_copies.append(send(tabs.at[to], tab_rx.at[d - 1], t_ss.at[d - 1], t_rs.at[d - 1], (lat, zh * 16 + to)))
 
+    pair_late.wait_recv()
+    add_pair(late, pair_l)
+    first_late = send_first(pair_l, a_l, al_ss, al_rs)
     for copy in first_early:
         copy.wait_recv()
     add_first(pair_e, a_e, acc_ae)
@@ -425,14 +444,6 @@
         copy.wait_recv()
     add_first(pair_l, a_l, acc_al)
     second_late = send_second(acc_al, b_l, bl_ss, bl_rs)
-
-    for copy in tab_copies:
-        copy.wait_recv()
-    total = tabs[plane]
-    for d in range(15):
-        total = total + tab_rx[d]
-    tab_sum[...] = total
-    tab_across = send(tab_sum, tab_pair, tp_ss, tp_rs, (lat, lax.rem(lon + 16, 32)))
 
     for copy in second_early:
         copy.wait_recv()
@@ -449,6 +460,14 @@
                 (lax.rem(to, 8) * 2 + core, (to // 8) * 16 + plane),
             )
         )
+
+    for copy in tab_copies:
+        copy.wait_recv()
+    total = tabs[plane]
+    for d in range(15):
+        total = total + tab_rx[d]
+    tab_sum[...] = total
+    tab_across = send(tab_sum, tab_pair, tp_ss, tp_rs, (lat, lax.rem(lon + 16, 32)))
 
     tab_across.wait_recv()
     tab_all[plane] = tab_sum[...] + tab_pair[...]
@@ -565,15 +584,20 @@
     def buf(*dims):
         return pltpu.VMEM(dims, f32)
 
+    arrays = (
+        fields.transpose(grid_order), cotangent.transpose(grid_order), region_ids.transpose(2, 0, 1),
+        *weights, order, rest, spread,
+    )
     tile = (8, 128)
     block = (12, 6, 2, C)
     packed = pl.pallas_call(
         functools.partial(kernel_a, lats, lons),
         out_shape=(shape(16, 8, 128), shape(*(HEADS, 1, 6336)), shape(*block), shape(*block)),
-        in_specs=[smem()] + [vmem()] * 18,
+        in_specs=[smem()] + [pl.BlockSpec(memory_space=pl.ANY)] * 18,
         out_specs=(vmem(),) * 4,
         scratch_shapes=[
-            buf(*block), buf(*block), buf(*block), buf(*block), buf(*block),
+            *[pltpu.VMEM(a.shape, a.dtype) for a in arrays], sems(18),
+            buf(*block), buf(*block), buf(*block), buf(*block), buf(*block), pltpu.VMEM((6, 2, 12), jnp.int32),
             buf(2, 4, 4, 2, 5, *tile), buf(2, 4, 4, 2, 3, *tile),
             buf(4, 4, 2, 5, *tile), buf(4, 4, 2, 3, *tile),
             buf(3, 4, 2, 5, *tile), buf(3, 4, 2, 3, *tile),
@@ -582,18 +606,15 @@
             buf(2, 8, *tile), buf(15, *tile), buf(*tile),
             buf(16, 24, 128), buf(15, 24, 128), buf(24, 128), buf(24, 128), buf(16, 24, 128), buf(3, 192, 128),
             buf(192, 384), buf(3, 192, 128), buf(HEADS, TOK, TOK), buf(3, 192, 128),
-            buf(256, 768), buf(256, 768), buf(768, 256), buf(8, 768), buf(2, 192, 128),
-            sems(3), sems(3), sems(3), sems(3), sems(3), sems(3),
+            buf(256, 768), buf(8, 768), buf(2, 192, 128),
+            sems(3), sems(3), sems(3), sems(3), one_sem, one_sem, sems(3), sems(3),
             one_sem, one_sem, one_sem, one_sem,
             sems(3), sems(3), sems(3), sems(3), sems(3), sems(3), sems(3), sems(3),
             sems(15), sems(15), sems(15), sems(15), sems(15), sems(15), one_sem, one_sem, sems(15), sems(15),
         ],
         compiler_params=pltpu.CompilerParams(collective_id=0, has_side_effects=True, vmem_limit_bytes=VMEM_LIMIT),
         name="block_both_ways",
-    )(
-        keep_mask, fields.transpose(grid_order), cotangent.transpose(grid_order), region_ids.transpose(2, 0, 1),
-        *weights, order, rest, spread,
-    )
+    )(keep_mask, *arrays)
     outs = list(
         pl.pallas_call(
             kernel_b,

time: 83.2 us -> 77.2 us (0.928)
  the two profiles are of different devices: /device:TPU:1 before, /device:TPU:21 now
where the time goes in v3:
time: 77.2 us; the launch traced here: 77.1 us
  Pallas kernels  76.4 us (99%)
    pallas_call x1, Pallas kernels, per_device(): pl.pallas_call(functools.partial(kernel_a, lats, lons), out_shape=(shape(...  74.5 us
    pallas_call x1, Pallas kernels, per_device(): pl.pallas_call(kernel_b, out_shape=(shape(2, *block), shape(C), shape(C),...  1.93 us

profile of v3, /device:TPU:21, one launch (start us, length us, event | category | flops | bytes accessed | tf_op | source)
XLA Modules:
  0.0 77.1 jit_solution(1162148143997945573)
XLA Ops:
  0.7 74.5 %block_both_ways.1 = (f32[16,8,128]{2,1,0:T(8,128)}, f32[6,1,6336]{2,1,0:T(1,128)}, f32[12,6,2,192]{3,2,1,0:T(2,128)}, f32[12,6,2,192]{3,2,1,0:T(2,128)}) custom-call(s32[2,2]{1,0:T(2,128)} %keep.3, f32[2,12,6,2,192]{4,3,2,1,0:T(2,128)} %bitcast.8, f32[2,12,6,2,192]{4,3,2,1,0:T(2,128)} %bitcast.9, s32[6,2,12]{2,1,0:T(2,128)} %bitcast.11, f32[192]{0:T(256)} %refs_3_.1, ...), custom_call_target="tpu_custom_call" | custom-call | tf_op jit(solution)/shard_map/block_both_ways/pallas_call | solution.py:593
  75.1 1.9 %unpack.1 = (f32[2,12,6,2,192]{4,3,2,1,0:T(2,128)}, f32[192]{0:T(256)}, f32[192]{0:T(256)}, f32[6,576]{1,0:T(8,128)}, f32[576]{0:T(1024)}, /*index=5*/f32[6,1,63...) custom-call(s32[2,2]{1,0:T(2,128)} %keep.3, ...), custom_call_target="tpu_custom_call" | custom-call | tf_op jit(solution)/shard_map/unpack/pallas_call | solution.py:619

commit v4 on v3

--- a/solution.py
+++ b/solution.py
@@ -63,8 +63,14 @@
     return lax.dot_general(a, b, (((ca,), (cb,)), ((), ())), preferred_element_type=f32)
 
 
-def product(a, b, ca=1, cb=0):
-    return one(a[0], b[0], ca, cb) + (one(a[0], b[1], ca, cb) + one(a[1], b[0], ca, cb))
+def product(a, b, cb=0):
+    rows = a[0].shape[0]
+    first = one(jnp.concatenate(a, axis=0), b[0], 1, cb)
+    return first[:rows] + (first[rows:] + one(a[0], b[1], 1, cb))
+
+
+def outer(a, b):
+    return one(a[0], b[0], 0, 0) + (one(a[0], b[1], 0, 0) + one(a[1], b[0], 0, 0))
 
 
 def norm_parts(values):
@@ -114,7 +120,7 @@
     load_sem, sel_x, sel_c, win_x, win_c, dxa, region_win,
     early, late, pair_e, pair_l, a_e, a_l, b_e, b_l, acc_ae, acc_al, acc_b, z_in, mine,
     tabs, tab_rx, tab_pair, tab_sum, tab_all, wide_s,
-    tab_in, bias_s, attn_s, diff_s, qp_s, row_s, tab_s,
+    tab_in, bias_s, attn_s, attn_hi, attn_lo, score_hi, score_lo, diff_s, qp_s, row_s, tab_s,
     hx_ss, hx_rs, hc_ss, hc_rs, reg_ss, reg_rs, back_ss, back_rs, pe_ss, pe_rs, pl_ss, pl_rs, ae_ss, ae_rs, al_ss, al_rs,
     be_ss, be_rs, bl_ss, bl_rs, z_ss, z_rs, g_ss, g_rs, t_ss, t_rs, tp_ss, tp_rs, tg_ss, tg_rs,
 ):
@@ -235,28 +241,38 @@
     gain1 = n1g[...].reshape(1, C)
     normed1 = halves(unit1 * gain1 + n1s[...].reshape(1, C))
     proj = product(normed1, w_qkv) + bqkv[...].reshape(1, 3 * C)
-    query = halves(proj[:, 0:C] * scale)
+    query_f = proj[:, 0:C] * scale
+    query = halves(query_f)
     key = halves(proj[:, C : 2 * C])
     value = halves(proj[:, 2 * C : 3 * C])
     lanes = lax.broadcasted_iota(jnp.int32, (1, C), 1)
     masks = [(lanes // 32 == h) for h in range(HEADS)]
 
-    def masked(pair, h):
+    def by_head(pair):
         zero = jnp.zeros((), bf16)
-        return tuple(jnp.where(masks[h], part, zero) for part in pair)
-
-    mixed = jnp.zeros((TOK, C), f32)
+        return tuple(jnp.concatenate([jnp.where(mask, part, zero) for mask in masks], axis=0) for part in pair)
+
+    def of_head(values, h):
+        return values[h * TOK : (h + 1) * TOK]
+
+    def own_lanes(values):
+        result = of_head(values, 0)
+        for h in range(1, HEADS):
+            result = jnp.where(masks[h], of_head(values, h), result)
+        return result
+
+    all_scores = product(by_head(query), key, 1)
     for h in range(HEADS):
-        scores = product(masked(query, h), key, 1, 1)
         strip = jnp.concatenate([bias_s[l, pl.ds(h, ZH, stride=8), :] for l in range(3)], axis=1)
         bias = jnp.concatenate(
             [pltpu.roll(strip, (384 - (5 - wn) * ZH) % 384, axis=1)[:, 0:TOK] for wn in range(6)], axis=0
         )
-        scores = jnp.where(same, scores + bias, -1e30)
+        scores = jnp.where(same, of_head(all_scores, h) + bias, -1e30)
         scores = jnp.exp(scores - jnp.max(scores, axis=-1, keepdims=True))
         attn = scores / jnp.sum(scores, axis=-1, keepdims=True)
         attn_s[h] = attn
-        mixed = mixed + product(halves(attn), masked(value, h))
+        attn_hi[h * TOK : (h + 1) * TOK, :], attn_lo[h * TOK : (h + 1) * TOK, :] = halves(attn)
+    mixed = own_lanes(product((attn_hi[...], attn_lo[...]), value))
     mixed = halves(mixed)
     branch = product(mixed, w_proj) + bproj[...].reshape(1, C)
 
@@ -274,7 +290,7 @@
     slope = cdf + hidden * jnp.exp(-0.5 * hidden * hidden) * (1.0 / math.sqrt(2.0 * math.pi))
     grad_y = halves(kept * cot_m)
     grad_hidden = halves(product(grad_y, w_out) * slope)
-    grad_out_w = product(halves(hidden * cdf), grad_y, 0, 0)
+    grad_out_w = outer(halves(hidden * cdf), grad_y)
 
     ones_lane = (lax.broadcasted_iota(jnp.int32, (1, 256), 1) & 7) == 6
 
@@ -283,7 +299,7 @@
         low = one(pair[1], spread[...], 1, 0)
         return jnp.where(ones_lane, 1.0, high).astype(bf16), low.astype(bf16)
 
-    grad_in_w = product(spread_out(normed2), grad_hidden, 0, 0)
+    grad_in_w = outer(spread_out(normed2), grad_hidden)
 
     low_lanes = lax.broadcasted_iota(jnp.int32, (8, 128), 1) < 64
 
@@ -312,7 +328,7 @@
     twin = (lat + 1 - 2 * core, lon)
     pair_early = send(early.at[1 - core], pair_e, pe_ss, pe_rs, twin)
 
-    grad_n2 = product(grad_hidden, w_in, 1, 1)
+    grad_n2 = product(grad_hidden, w_in, 1)
     row_s[0:1, 2 * C : 3 * C] = jnp.sum(grad_n2 * unit2, axis=0, keepdims=True)
     row_s[0:1, 3 * C : 4 * C] = jnp.sum(grad_n2, axis=0, keepdims=True)
     grad_m = cot_m + norm_back(grad_n2, gain2, unit2, inv2)
@@ -355,23 +371,25 @@
         return copies
 
     grad_b = halves(kept * grad_a)
-    qp_s[:, 3 * C : 4 * C] = product(spread_out(mixed), grad_b, 0, 0)
-    grad_o = halves(product(grad_b, w_proj, 1, 1))
-    grad_q = jnp.zeros((TOK, C), f32)
-    grad_k = jnp.zeros((TOK, C), f32)
-    grad_v = jnp.zeros((TOK, C), f32)
+    qp_s[:, 3 * C : 4 * C] = outer(spread_out(mixed), grad_b)
+    grad_o = product(grad_b, w_proj, 1)
+    grad_o_t = halves(grad_o.T)
+    query_t = halves(query_f.T)
+    all_grad = product(by_head(halves(grad_o)), value, 1)
     diff_s[...] = jnp.zeros(diff_s.shape, f32)
     first_early = None
+    grad_v = []
+    grad_k = []
     for h in range(HEADS):
         attn = attn_s[h]
-        grad_oh = masked(grad_o, h)
-        grad_attn = product(grad_oh, value, 1, 1)
-        grad_v = grad_v + product(halves(attn), grad_oh, 0, 0)
-        term = attn * grad_attn
+        term = attn * of_head(all_grad, h)
         grad_s = term - attn * jnp.sum(term, axis=-1, keepdims=True)
         grad_sp = halves(grad_s)
-        grad_q = grad_q + product(grad_sp, masked(key, h))
-        grad_k = grad_k + product(grad_sp, masked(query, h), 0, 0)
+        rows = slice(h * TOK, (h + 1) * TOK)
+        score_hi[rows, :], score_lo[rows, :] = grad_sp
+        head = slice(h * 32, h * 32 + 32)
+        grad_v.append(product(tuple(part[head, :] for part in grad_o_t), (attn_hi[rows, :], attn_lo[rows, :])))
+        grad_k.append(product(tuple(part[head, :] for part in query_t), grad_sp))
         wide = jnp.concatenate([grad_s, jnp.zeros((TOK, 384 - TOK), f32)], axis=1)
         total = None
         for wn in range(6):
@@ -385,9 +403,12 @@
             pair_early.wait_recv()
             add_pair(early, pair_e)
             first_early = send_first(pair_e, a_e, ae_ss, ae_rs)
+    grad_q = own_lanes(product((score_hi[...], score_lo[...]), key))
+    grad_k = jnp.concatenate(grad_k, axis=0).T
+    grad_v = jnp.concatenate(grad_v, axis=0).T
     grad_p = halves(jnp.concatenate([grad_q * scale, grad_k, grad_v], axis=1))
-    qp_s[:, 0 : 3 * C] = product(spread_out(normed1), grad_p, 0, 0)
-    grad_n1 = product(grad_p, w_qkv, 1, 1)
+    qp_s[:, 0 : 3 * C] = outer(spread_out(normed1), grad_p)
+    grad_n1 = product(grad_p, w_qkv, 1)
     row_s[0:1, 0:C] = jnp.sum(grad_n1 * unit1, axis=0, keepdims=True)
     row_s[0:1, C : 2 * C] = jnp.sum(grad_n1, axis=0, keepdims=True)
 
@@ -488,8 +509,24 @@
     gather[slot] = total
     g_copies = []
     for d in range(1, 16):
-        to = lax.rem(lat + d, 16)
-        g_copies.append(send(mine, gather.at[slot], g_ss.at[d - 1], g_rs.at[d - 1], (to, lon)))
+        g_copies.append(
+            pltpu.make_async_remote_copy(
+                src_ref=mine, dst_ref=gather.at[slot], send_sem=g_ss.at[d - 1], recv_sem=g_rs.at[d - 1],
+                device_id=(lax.rem(lat + d, 16), lon), device_id_type=MESH,
+            )
+        )
+    every.extend(g_copies)
+
+    @pl.when(zl < 4)
+    def _():
+        for copy in reversed(g_copies):
+            copy.start()
+
+    @pl.when(zl >= 4)
+    def _():
+        for copy in g_copies:
+            copy.start()
+
 
     for copy in tab_back:
         copy.wait_recv()
@@ -605,7 +642,8 @@
             buf(4, 2, 5, *tile), buf(4, 2, 3, *tile),
             buf(2, 8, *tile), buf(15, *tile), buf(*tile),
             buf(16, 24, 128), buf(15, 24, 128), buf(24, 128), buf(24, 128), buf(16, 24, 128), buf(3, 192, 128),
-            buf(192, 384), buf(3, 192, 128), buf(HEADS, TOK, TOK), buf(3, 192, 128),
+            buf(192, 384), buf(3, 192, 128), buf(HEADS, TOK, TOK),
+            *[pltpu.VMEM((HEADS * TOK, TOK), bf16)] * 4, buf(3, 192, 128),
             buf(256, 768), buf(8, 768), buf(2, 192, 128),
             sems(3), sems(3), sems(3), sems(3), one_sem, one_sem, sems(3), sems(3),
             one_sem, one_sem, one_sem, one_sem,

time: 77.2 us -> 77.4 us (level)
  no operation moved by 1% of the time
where the time goes in v4:
time: 77.4 us; the launch traced here: 77.3 us
  Pallas kernels  76.6 us (99%)
    pallas_call x1, Pallas kernels, per_device(): pl.pallas_call(functools.partial(kernel_a, lats, lons), out_shape=(shape(...  74.7 us
    pallas_call x1, Pallas kernels, per_device(): pl.pallas_call(kernel_b, out_shape=(shape(2, *block), shape(C), shape(C),...  1.93 us

profile of v4, /device:TPU:21, one launch (start us, length us, event | category | flops | bytes accessed | tf_op | source)
XLA Modules:
  0.0 77.3 jit_solution(8421969261990140267)
XLA Ops:
  0.7 74.7 %block_both_ways.1 = (f32[16,8,128]{2,1,0:T(8,128)}, f32[6,1,6336]{2,1,0:T(1,128)}, f32[12,6,2,192]{3,2,1,0:T(2,128)}, f32[12,6,2,192]{3,2,1,0:T(2,128)}) custom-call(s32[2,2]{1,0:T(2,128)} %keep.3, f32[2,12,6,2,192]{4,3,2,1,0:T(2,128)} %bitcast.8, f32[2,12,6,2,192]{4,3,2,1,0:T(2,128)} %bitcast.9, s32[6,2,12]{2,1,0:T(2,128)} %bitcast.11, f32[192]{0:T(256)} %refs_3_.1, ...), custom_call_target="tpu_custom_call" | custom-call | tf_op jit(solution)/shard_map/block_both_ways/pallas_call | solution.py:630
  75.3 1.9 %unpack.1 = (f32[2,12,6,2,192]{4,3,2,1,0:T(2,128)}, f32[192]{0:T(256)}, f32[192]{0:T(256)}, f32[6,576]{1,0:T(8,128)}, f32[576]{0:T(1024)}, /*index=5*/f32[6,1,63...) custom-call(s32[2,2]{1,0:T(2,128)} %keep.3, ...), custom_call_target="tpu_custom_call" | custom-call | tf_op jit(solution)/shard_map/unpack/pallas_call | solution.py:657
